TPU v7x, 256 devices: a whole 4x4x8 slice. The times are simulated.
256 devices in a mesh: var: 8 (over y_hi, x), lat: 16 (over z, y_lo), dp: 2 (over core).
Axes of the slice: x: 4, y: 4 (y_hi: 2, y_lo: 2; y = y_hi * 2 + y_lo), z: 8, core: 2. Of those that a mesh axis runs over, the one named last changes fastest.
Arguments:
- patches: bfloat16 [16, 96, 7680], P(('dp', 'var'), 'lat'), parts along dimension 0, may hold values from -6 to 6
- level_bias: bfloat16 [8, 512], replicated, may hold values from -6 to 6
- embed_weight: bfloat16 [80, 512], replicated, may hold values from -0.625 to 0.625
- latent_query: bfloat16 [3, 512], replicated, may hold values from -60 to 60
- cross_key: bfloat16 [512, 512], replicated, may hold values from -0.25 to 0.25
- cross_value: bfloat16 [512, 512], replicated, may hold values from -0.25 to 0.25
- cross_output: bfloat16 [512, 512], replicated, may hold values from -0.25 to 0.25
- first_gain: float32 [512], replicated, may hold values from 0.1 to 1.9
- window_query: bfloat16 [512, 512], replicated, may hold values from -2 to 2
- window_context: bfloat16 [512, 1024], replicated, may hold values from -0.25 to 0.25
- window_output: bfloat16 [512, 512], replicated, may hold values from -0.25 to 0.25
- second_gain: float32 [512], replicated, may hold values from 0.1 to 1.9
- up_weight: bfloat16 [512, 2048], replicated, may hold values from -0.25 to 0.25
- down_weight: bfloat16 [2048, 512], replicated, may hold values from -0.125 to 0.125
Outputs:
- encoded: bfloat16 [6, 96, 96, 512], P('dp', 'lat', 'var'), parts along dimension 0
There are 2 independent parts, one for each index of `dp`. A program takes and returns all parts, laid end to end along the dimension named above; an argument that names none is the same for every part. Nothing has to cross between parts.
All inputs are finite; a program needn't handle non-finite values.
Results may differ from a plain program's by a relative error of at most 0.013.
Values may be sent and summed in bfloat16 or wider, within the bound.
No kernel may reach another device: no remote copies, remote signals or barrier semaphores. Data moves between devices by JAX's collectives and lax.ppermute only.
A program may use at most 64 MiB of HBM per device.

v0:
```python
import jax
import jax.numpy as jnp
from jax import lax
from jax.sharding import Mesh
from jax.sharding import PartitionSpec as P

HEADS = 16
WLAT = 6
WLON = 12
SHIFT = 3
VAR = ("var_0", "var_1")
DP_VAR = ("dp", "var_0", "var_1")


epsilon = 1e-05
masked_score = -1e30


def in_blocks(array, dim, count):
    before, after = (array.shape[:dim], array.shape[dim + 1 :])
    return jnp.moveaxis(array.reshape(*before, count, -1, *after), dim, 0)


def in_order(parts, dim):
    lengths = list(parts.shape[1:])
    lengths[dim] *= parts.shape[0]
    return jnp.moveaxis(parts, 0, dim).reshape(lengths)


def moved_by_axis(parts, axes, sequence):
    lengths = [lax.axis_size(a) for a in axes]
    parts = parts.reshape(*lengths, *parts.shape[1:])
    for k in sequence:
        parts = lax.all_to_all(parts, axes[k], split_axis=k, concat_axis=k, tiled=True)
    return parts.reshape(-1, *parts.shape[len(axes) :])


def exchange_by_axis(array, axes, sequence, split_dim, concat_dim):
    parts = in_blocks(array, split_dim, lax.axis_size(axes))
    return in_order(moved_by_axis(parts, axes, sequence), concat_dim)


def with_halo(block, sides, width):
    for axis, dim in sides:
        count = lax.axis_size(axis)
        forward = [(i, i + 1) for i in range(count - 1)]
        backward = [(target, source) for source, target in forward]
        low = lax.ppermute(
            lax.slice_in_dim(block, block.shape[dim] - width, None, axis=dim), axis, forward
        )
        high = lax.ppermute(lax.slice_in_dim(block, 0, width, axis=dim), axis, backward)
        block = jnp.concatenate([low, block, high], axis=dim)
    return block


def layer_norm(tensor, scales):
    center = jnp.mean(tensor, axis=-1, keepdims=True)
    offset = tensor - center
    spread = jnp.mean(offset * offset, axis=-1, keepdims=True)
    return offset * lax.rsqrt(spread + epsilon) * scales


def level_partials(pixels, biases, embed_weight, latent_query, cross_key, cross_value):
    level_count, row_count, flat_cols = pixels.shape
    pixel_count, channels = embed_weight.shape
    col_count = flat_cols // pixel_count
    head_size = channels // HEADS
    latent_count = latent_query.shape[0]
    embedded = jnp.dot(
        pixels.reshape(-1, pixel_count), embed_weight, preferred_element_type=jnp.float32
    )
    embedded = embedded.reshape(level_count, -1, channels) + biases.astype(jnp.float32)[:, None, :]
    embedded = embedded.astype(jnp.bfloat16).reshape(-1, channels)
    head_shape = (level_count, row_count, col_count, HEADS, head_size)
    key_rows = (
        jnp.dot(embedded, cross_key, preferred_element_type=jnp.float32)
        .astype(jnp.bfloat16)
        .reshape(head_shape)
    )
    value_rows = (
        jnp.dot(embedded, cross_value, preferred_element_type=jnp.float32)
        .astype(jnp.bfloat16)
        .reshape(head_shape)
    )
    queries = latent_query.reshape(latent_count, HEADS, head_size)
    scores = jnp.einsum(
        "lrwhc,qhc->qrwhl", key_rows, queries, preferred_element_type=jnp.float32
    ) * head_size ** (-0.5)
    maxima = jnp.max(scores, axis=-1)
    weights = jnp.exp(scores - maxima[..., None])
    totals = jnp.sum(weights, axis=-1)
    weighted = jnp.einsum(
        "qrwhl,lrwhc->qrwhc",
        weights,
        value_rows.astype(jnp.float32),
        precision=lax.Precision.HIGHEST,
    )
    return (maxima, totals, weighted)


def window_attend(query_rows, context_rows, valid_rows):
    level_count, row_count, col_count, channels = query_rows.shape
    head_size = channels // HEADS

    def windows_of(tensor):
        blocks = tensor.reshape(
            level_count, row_count // WLAT, WLAT, col_count // WLON, WLON, HEADS, head_size
        )
        blocks = blocks.transpose(1, 3, 0, 2, 4, 5, 6)
        return blocks.reshape(-1, level_count * WLAT * WLON, HEADS, head_size)

    queries = windows_of(query_rows)
    key_rows = windows_of(context_rows[..., :channels])
    value_rows = windows_of(context_rows[..., channels:])
    window_mask = jnp.broadcast_to(
        valid_rows.reshape(row_count // WLAT, 1, 1, WLAT, 1),
        (row_count // WLAT, col_count // WLON, level_count, WLAT, WLON),
    ).reshape(-1, level_count * WLAT * WLON)
    scores = jnp.einsum(
        "bthc,bshc->bhts", queries, key_rows, preferred_element_type=jnp.float32
    ) * head_size ** (-0.5)
    scores = jnp.where(window_mask[:, None, None, :], scores, masked_score)
    highest = jnp.max(scores, axis=-1, keepdims=True)
    weights = jnp.exp(scores - highest)
    shares = (weights / jnp.sum(weights, axis=-1, keepdims=True)).astype(jnp.bfloat16)
    attended = jnp.einsum(
        "bhts,bshc->bthc", shares, value_rows, preferred_element_type=jnp.float32
    ).astype(jnp.bfloat16)
    attended = attended.reshape(
        row_count // WLAT, col_count // WLON, level_count, WLAT, WLON, channels
    )
    return attended.transpose(2, 0, 3, 1, 4, 5).reshape(level_count, row_count, col_count, channels)


def body(
    patches,
    level_bias,
    embed_weight,
    latent_query,
    cross_key,
    cross_value,
    cross_output,
    first_gain,
    window_query,
    window_context,
    window_output,
    second_gain,
    up_weight,
    down_weight,
):
    level_here, row_count, flat_cols = patches.shape
    pixel_count, channels = embed_weight.shape
    latent_count = latent_query.shape[0]
    lon_local = flat_cols // pixel_count // lax.axis_size(VAR)
    gathered = exchange_by_axis(patches, VAR, (0, 1), 2, 0)
    maxima, totals, weighted = level_partials(
        gathered, level_bias, embed_weight, latent_query, cross_key, cross_value
    )
    pooled = weighted / totals[..., None]
    grid_shape = (latent_count, row_count, lon_local, channels)
    latent = jnp.dot(
        pooled.astype(jnp.bfloat16).reshape(-1, channels),
        cross_output,
        preferred_element_type=jnp.float32,
    ).reshape(grid_shape)
    latent = (latent + latent_query.astype(jnp.float32)[:, None, None, :]).astype(jnp.bfloat16)
    normed = layer_norm(latent.astype(jnp.float32), first_gain).astype(jnp.bfloat16)
    flat_normed = normed.reshape(-1, channels)
    query_rows = (
        jnp.dot(flat_normed, window_query, preferred_element_type=jnp.float32)
        .astype(jnp.bfloat16)
        .reshape(grid_shape)
    )
    widened = with_halo(normed, (("lat", 1),), SHIFT)
    context = (
        jnp.dot(widened.reshape(-1, channels), window_context, preferred_element_type=jnp.float32)
        .astype(jnp.bfloat16)
        .reshape(latent_count, row_count + 2 * SHIFT, lon_local, 2 * channels)
    )
    padded_query = jnp.pad(query_rows, ((0, 0), (SHIFT, SHIFT), (0, 0), (0, 0)))
    row_ids = (
        lax.axis_index("lat") * row_count
        - SHIFT
        + jnp.arange(row_count + 2 * SHIFT, dtype=jnp.int32)
    )
    valid_rows = (row_ids >= 0) & (row_ids < row_count * lax.axis_size("lat"))
    attended = window_attend(padded_query, context, valid_rows)[:, SHIFT : SHIFT + row_count]
    mixed_rows = jnp.dot(
        attended.reshape(-1, channels), window_output, preferred_element_type=jnp.float32
    ) + latent.astype(jnp.float32).reshape(-1, channels)
    second = layer_norm(mixed_rows, second_gain).astype(jnp.bfloat16)
    hidden = jax.nn.gelu(jnp.dot(second, up_weight, preferred_element_type=jnp.float32)).astype(
        jnp.bfloat16
    )
    result = mixed_rows + jnp.dot(hidden, down_weight, preferred_element_type=jnp.float32)
    return result.reshape(grid_shape).astype(jnp.bfloat16)


def solution(mesh):
    finer = Mesh(
        mesh.devices.reshape(2, 4, mesh.shape["lat"], mesh.shape["dp"]),
        ("var_0", "var_1", "lat", "dp"),
    )
    placed = (
        P(DP_VAR, "lat", None),
        P(),
        P(),
        P(),
        P(),
        P(),
        P(),
        P(),
        P(),
        P(),
        P(),
        P(),
        P(),
        P(),
    )
    return jax.shard_map(
        body, mesh=finer, in_specs=placed, out_specs=P("dp", "lat", VAR, None), check_vma=False
    )
```

profile of v0, /device:TPU:104, one launch (start us, length us, event | category | flops | bytes accessed | tf_op | source)
XLA Modules:
  0.0 108.3 jit_solution(17676725315419019195)
XLA Ops:
  0.0 1.2 %reshape.118 = bf16[1,6,8,960]{3,2,1,0:T(8,128)(2,1)S(1)} reshape(bf16[1,6,7680]{2,1,0:T(8,128)(2,1)} %param.14) | data formatting | bytes 184320 | tf_op jit(solution)/shard_map/reshape | solution.py:21
  1.3 0.7 copy.68
  1.9 3.6 %all-to-all-start = ((bf16[2,4,1,6,960]{4,1,3,2,0:T(4,128)(2,1)}), bf16[2,4,1,6,960]{4,1,3,2,0:T(4,128)(2,1)S(1)}, u32[]{:S(2)}, u32[]{:S(2)}) async-start(bf16[2,4,1,6,960]{4,1,3,2,0:T(4,128)(2,1)} %copy.68), calls=%async_computation | async-start | bytes 196608 | tf_op jit(solution)/shard_map/all_to_all | solution.py:34
  5.5 0.7 convert_element_type.63
  6.2 0.8 reshape.123
  7.0 0.7 convert_element_type.58
  7.7 3.6 %all-to-all-done = bf16[2,4,1,6,960]{4,1,3,2,0:T(4,128)(2,1)S(1)} async-done(((bf16[2,4,1,6,960]{4,1,3,2,0:T(4,128)(2,1)}), bf16[2,4,1,6,960]{4,1,3,2,0:T(4,128)(2,1)S(1)}, u32[]{:S(2)}, u32[]{:S(2)}) %all-to-all-start) | async-done | bytes 92192 | tf_op jit(solution)/shard_map/all_to_all | solution.py:34
  11.3 0.7 copy.69
  12.0 4.3 %all-to-all-start.1 = ((bf16[2,4,1,6,960]{4,0,3,2,1:T(2,128)(2,1)}), bf16[2,4,1,6,960]{4,0,3,2,1:T(2,128)(2,1)S(1)}, u32[]{:S(2)}, u32[]{:S(2)}) async-start(bf16[2,4,1,6,960]{4,0,3,2,1:T(2,128)(2,1)} %copy.69), calls=%async_computation.1 | async-start | bytes 196608 | tf_op jit(solution)/shard_map/all_to_all | solution.py:34
  16.3 0.1 broadcast_in_dim.12
  16.4 0.1 broadcast_in_dim.13
  16.5 5.6 %all-to-all-done.1 = bf16[2,4,1,6,960]{4,0,3,2,1:T(2,128)(2,1)S(1)} async-done(((bf16[2,4,1,6,960]{4,0,3,2,1:T(2,128)(2,1)}), bf16[2,4,1,6,960]{4,0,3,2,1:T(2,128)(2,1)S(1)}, u32[]{:S(2)}, u32[]{:S(2)}) %all-to-all-start.1) | async-done | bytes 92192 | tf_op jit(solution)/shard_map/all_to_all | solution.py:34
  22.2 0.2 dot_general.43
  22.4 0.0 copy-done.5
  22.4 0.3 fusion.27
  22.7 1.5 %convolution_convert_fusion.1 = bf16[576,512]{1,0:T(8,128)(2,1)S(1)} fusion(bf16[576,512]{1,0:T(8,128)(2,1)S(1)} %bitcast.65, bf16[512,512]{1,0:T(8,128)(2,1)} %param.18), kind=kOutput, calls=%fused_computation.35 | convolution fusion | flops 302284800 | bytes 1703936 | tf_op jit(solution)/shard_map/dot_general | solution.py:76
  24.2 2.4 %reshape.122 = bf16[8,6,12,16,32]{4,3,2,1,0:T(8,128)(2,1)} reshape(bf16[576,512]{1,0:T(8,128)(2,1)S(1)} %convolution_convert_fusion.1) | data formatting | bytes 1179648 | tf_op jit(solution)/shard_map/reshape | solution.py:78
  26.6 9.2 %bitcast_reduce_fusion = (f32[3,6,12,16]{2,0,1,3:T(4,128)S(1)}, f32[16,8,6,12,3]{3,4,2,1,0:T(4,128)S(1)}) fusion(bf16[3,16,32,1,1]{2,1,0,4,3:T(8,128)(2,1)S(1)} %bitcast.71, bf16[8,6,12,16,32]{4,3,2,1,0:T(8,128)(2,1)} %reshape.122), kind=kOutput, calls=%fused_computation.29 | convolution fusion | flops 1821312 | bytes 717312 | tf_op jit(solution)/shard_map/lrwhc,qhc->qrwhl/dot_general | solution.py:86
  35.8 1.9 %fusion.60 = (f32[3,6,12,16]{2,0,1,3:T(4,128)S(1)}, f32[3,6,12,16,8]{2,0,1,4,3:T(4,128)}) fusion(f32[3,6,12,16]{2,0,1,3:T(4,128)S(1)} %get-tuple-element.11, f32[16,8,6,12,3]{3,4,2,1,0:T(4,128)S(1)} %get-tuple-element.12), kind=kLoop, calls=%fused_computation.73 | loop fusion | flops 51840 | bytes 248832 | tf_op jit(solution)/shard_map/reduce_sum | solution.py:91
  37.7 5.3 %copy.74 = f32[3,6,12,16,8]{4,0,3,2,1:T(4,128)} copy(f32[3,6,12,16,8]{2,0,1,4,3:T(4,128)} %get-tuple-element.6) | data formatting | bytes 221184 | tf_op jit(solution)/shard_map/exp | solution.py:90
  43.0 1.5 %convolution_convert_fusion.2 = bf16[576,512]{1,0:T(8,128)(2,1)S(1)} fusion(bf16[576,512]{1,0:T(8,128)(2,1)S(1)} %bitcast.66, bf16[512,512]{1,0:T(8,128)(2,1)} %param.19), kind=kOutput, calls=%fused_computation.36 | convolution fusion | flops 302284800 | bytes 1703936 | tf_op jit(solution)/shard_map/dot_general | solution.py:81
  44.5 2.4 %reshape.121 = bf16[8,6,12,16,32]{4,3,2,1,0:T(8,128)(2,1)} reshape(bf16[576,512]{1,0:T(8,128)(2,1)S(1)} %convolution_convert_fusion.2) | data formatting | bytes 1179648 | tf_op jit(solution)/shard_map/reshape | solution.py:83
  46.8 0.7 copy.75
  47.6 7.7 %fusion.10 = bf16[3,6,12,16,32]{4,0,3,2,1:T(4,128)(2,1)S(1)} fusion(f32[3,6,12,16,8]{4,0,3,2,1:T(4,128)} %copy.74, bf16[8,6,12,16,32]{4,3,2,1,0:T(8,128)(2,1)} %reshape.121, f32[3,6,12,16]{0,3,2,1:T(8,128)S(1)} %copy.75), kind=kOutput, calls=%fused_computation.15 | convolution fusion | flops 10838016 | bytes 935424 | tf_op jit(solution)/shard_map/qrwhl,lrwhc->qrwhc/dot_general | solution.py:92
  55.3 0.2 copy.76
  55.5 0.0 copy-start.6
  55.5 0.8 dot_general.49
  56.3 1.4 %fusion.64 = (f32[3,6,12]{2,1,0:T(8,128)S(1)}, f32[3,6,12,512]{3,2,1,0:T(8,128)S(1)}) fusion(f32[3,512]{1,0:T(4,128)S(1)} %convert_element_type.63, bf16[3,6,12,512]{3,2,1,0:T(8,128)(2,1)S(1)} %dot_general.49, bf16[512,512]{1,0:T(8,128)(2,1)} %param.20), kind=kOutput, calls=%fused_computation.76 | convolution fusion | flops 113688360 | bytes 1194848 | tf_op jit(solution)/shard_map/dot_general | solution.py:161
  57.8 0.2 multiply_reduce_fusion
  58.0 0.2 multiply_convert_fusion
  58.2 0.7 fusion.63
  58.9 0.1 reshape.128
  59.0 3.3 %collective-permute-start.1 = (bf16[3,3,12,512]{3,2,1,0:T(8,128)(2,1)}, bf16[3,3,12,512]{3,2,1,0:T(8,128)(2,1)}, u32[]{:S(2)}, u32[]{:S(2)}) collective-permute-start(bf16[3,3,12,512]{3,2,1,0:T(8,128)(2,1)} %get-tuple-element.10), channel_id=1, source_target_pairs={{2,0},{4,2},{6,4},{8,6},{10,8},{12,10},{14,12},{16,14},{18,16},{20... | collective-permute-start | bytes 331784 | tf_op jit(solution)/shard_map/ppermute | solution.py:51
  62.2 4.7 %collective-permute-start = (bf16[3,3,12,512]{3,2,1,0:T(8,128)(2,1)}, bf16[3,3,12,512]{3,2,1,0:T(8,128)(2,1)}, u32[]{:S(2)}, u32[]{:S(2)}) collective-permute-start(bf16[3,3,12,512]{3,2,1,0:T(8,128)(2,1)} %get-tuple-element.9), channel_id=1, source_target_pairs={{0,2},{2,4},{4,6},{6,8},{8,10},{10,12},{12,14},{14,16},{16,18},{18... | collective-permute-start | bytes 331784 | tf_op jit(solution)/shard_map/ppermute | solution.py:48
  66.9 1.3 %convolution_convert_fusion.3 = bf16[216,512]{1,0:T(8,128)(2,1)S(1)} fusion(bf16[216,512]{1,0:T(8,128)(2,1)S(1)} %reshape.128, bf16[512,512]{1,0:T(8,128)(2,1)} %param.22), kind=kOutput, calls=%fused_computation.45 | convolution fusion | flops 113356800 | bytes 966656 | tf_op jit(solution)/shard_map/dot_general | solution.py:170
  68.3 0.8 reshape.137
  69.1 0.1 reshape.129
  69.1 0.1 pad.4
  69.2 2.2 %reshape.130 = bf16[3,2,6,1,12,16,32]{6,5,4,2,1,0,3:T(8,128)(2,1)} reshape(bf16[3,12,12,512]{3,2,1,0:T(8,128)(2,1)S(1)} %pad.4) | data formatting | bytes 884736 | tf_op jit(solution)/shard_map/reshape | solution.py:106
  71.4 3.1 %copy.78 = bf16[2,1,3,6,12,16,32]{6,5,4,3,2,0,1:T(8,128)(2,1)} copy(bf16[2,1,3,6,12,16,32]{6,5,4,3,0,2,1:T(8,128)(2,1)} %bitcast.60) | data formatting | bytes 884736 | tf_op jit(solution)/shard_map/transpose | solution.py:109
  74.5 0.0 collective-permute-done.1
  74.5 0.0 collective-permute-done
  74.5 1.1 pad_maximum_fusion
  75.6 0.1 reshape.124
  75.7 2.8 %convolution_convert_fusion = bf16[432,1024]{1,0:T(8,128)(2,1)} fusion(bf16[432,512]{1,0:T(8,128)(2,1)S(1)} %reshape.124, bf16[512,1024]{1,0:T(8,128)(2,1)} %param.23), kind=kOutput, calls=%fused_computation.32 | convolution fusion | flops 453427200 | bytes 2375680 | tf_op jit(solution)/shard_map/dot_general | solution.py:176
  78.5 1.3 %reshape.125 = bf16[3,12,12,1024]{3,2,1,0:T(8,128)(2,1)S(1)} reshape(bf16[432,1024]{1,0:T(8,128)(2,1)} %convolution_convert_fusion) | data formatting | bytes 1769472 | tf_op jit(solution)/shard_map/reshape | solution.py:178
  79.8 1.2 %fusion.62 = (bf16[3,12,12,512]{3,2,1,0:T(8,128)(2,1)}, bf16[3,12,12,512]{3,2,1,0:T(8,128)(2,1)}) fusion(bf16[3,12,12,1024]{3,2,1,0:T(8,128)(2,1)S(1)} %reshape.125), kind=kLoop, calls=%fused_computation.74 | loop fusion | bytes 1769472 | tf_op jit(solution)/shard_map/slice | solution.py:114
  81.0 3.3 %reshape.132 = bf16[3,2,6,1,12,16,32]{6,5,4,2,1,0,3:T(8,128)(2,1)} reshape(bf16[3,12,12,512]{3,2,1,0:T(8,128)(2,1)} %get-tuple-element.8) | data formatting | bytes 884736 | tf_op jit(solution)/shard_map/reshape | solution.py:106
  84.3 3.2 %copy.79 = bf16[2,1,3,6,12,16,32]{6,5,4,3,2,0,1:T(8,128)(2,1)} copy(bf16[2,1,3,6,12,16,32]{6,5,4,3,0,2,1:T(8,128)(2,1)} %bitcast.61) | data formatting | bytes 884736 | tf_op jit(solution)/shard_map/transpose | solution.py:109
  87.5 2.0 %reshape.126 = bf16[3,2,6,1,12,16,32]{6,5,4,2,1,0,3:T(8,128)(2,1)} reshape(bf16[3,12,12,512]{3,2,1,0:T(8,128)(2,1)S(1)} %copy-done.3) | data formatting | bytes 884736 | tf_op jit(solution)/shard_map/reshape | solution.py:106
  89.4 2.1 %copy.77 = bf16[2,1,3,6,12,16,32]{6,5,4,3,2,0,1:T(8,128)(2,1)S(1)} copy(bf16[2,1,3,6,12,16,32]{6,5,4,3,0,2,1:T(8,128)(2,1)} %bitcast.62) | data formatting | bytes 884736 | tf_op jit(solution)/shard_map/transpose | solution.py:109
  91.5 0.5 copy-done.2
  92.0 1.2 %fusion.20 = f32[2,16,216,216]{2,3,1,0:T(8,128)S(1)} fusion(bf16[2,216,16,32]{3,2,1,0:T(8,128)(2,1)S(1)} %bitcast.64, bf16[2,216,16,32]{3,2,1,0:T(8,128)(2,1)S(1)} %bitcast.63), kind=kOutput, calls=%fused_computation.25 | convolution fusion | flops 95551488 | bytes 6856704 | tf_op jit(solution)/shard_map/bthc,bshc->bhts/dot_general | solution.py:119
  93.1 3.0 %fusion.65 = (f32[2,16,216]{2,1,0:T(8,128)S(1)}, f32[2,16,216,216]{2,3,1,0:T(8,128)S(1)}) fusion(f32[2,16,216,216]{2,3,1,0:T(8,128)S(1)} %fusion.20, pred[2,216]{1,0:T(4,128)(4,1)S(1)} %broadcast_in_dim.13), kind=kOutput, calls=%fused_computation.77 | output fusion | flops 8958167 | bytes 11972016 | tf_op jit(solution)/shard_map/sub | solution.py:124
  96.2 0.9 fusion.33
  97.0 2.4 %copy.84 = bf16[2,216,16,32]{3,2,0,1:T(8,128)(2,1)} copy(bf16[2,216,16,32]{1,3,2,0:T(8,128)(2,1)S(1)} %fusion.33) | data formatting | bytes 884736 | tf_op jit(solution)/shard_map/convert_element_type | solution.py:128
  99.4 3.2 %reshape.134 = bf16[2,1,3,6,12,512]{5,0,4,3,2,1:T(2,128)(2,1)S(1)} reshape(bf16[2,216,16,32]{3,2,0,1:T(8,128)(2,1)} %copy.84) | data formatting | bytes 884736 | tf_op jit(solution)/shard_map/reshape | solution.py:129
  102.7 0.1 copy.85
  102.8 0.0 copy-start.7
  102.8 0.1 reshape.136
  102.9 1.4 %fusion.66 = (f32[216]{0:T(256)S(1)}, f32[216,512]{1,0:T(8,128)S(1)}) fusion(f32[216,512]{1,0:T(8,128)S(1)} %copy-done.4, bf16[216,512]{1,0:T(8,128)(2,1)S(1)} %reshape.136, bf16[512,512]{1,0:T(8,128)(2,1)} %param.24), kind=kOutput, calls=%fused_computation.78 | convolution fusion | flops 113467176 | bytes 1631072 | tf_op jit(solution)/shard_map/dot_general | solution.py:188
  104.3 0.2 multiply_reduce_fusion.1
  104.5 3.0 %fusion.38 = bf16[216,512]{1,0:T(8,128)(2,1)S(1)} fusion(f32[216,512]{1,0:T(8,128)S(1)} %get-tuple-element.18, bf16[2048,512]{1,0:T(8,128)(2,1)S(1)} %copy-done, bf16[512,2048]{1,0:T(8,128)(2,1)} %param.26, f32[512]{0:T(512)S(1)} %copy-done.7, f32[216]{0:T(256)S(1)} %add_rsqrt_fusion.1, f32[216]{0:T(256)S(1)} %broadcast_multiply_fusion.1), kind=kOutput, calls=%fused_computation.44 | convolution fusion | flops 910614528 | bytes 4861632 | tf_op jit(solution)/shard_map/dot_general | solution.py:195
  107.5 0.8 convert_element_type.75
  (20 shorter events, 0.1 us)
Async XLA Ops:
  0.0 104.5 %copy-start = (bf16[2048,512]{1,0:T(8,128)(2,1)S(1)}, bf16[2048,512]{1,0:T(8,128)(2,1)}, u32[]{:S(2)}) copy-start(bf16[2048,512]{1,0:T(8,128)(2,1)} %param.27) | copy-start | bytes 6291460
  0.0 22.4 %copy-start.5 = (bf16[80,512]{1,0:T(8,128)(2,1)S(1)}, bf16[80,512]{1,0:T(8,128)(2,1)}, u32[]{:S(2)}) copy-start(bf16[80,512]{1,0:T(8,128)(2,1)} %param.16) | copy-start | bytes 245764
  1.9 9.4 %all-to-all-start = ((bf16[2,4,1,6,960]{4,1,3,2,0:T(4,128)(2,1)}), bf16[2,4,1,6,960]{4,1,3,2,0:T(4,128)(2,1)S(1)}, u32[]{:S(2)}, u32[]{:S(2)}) async-start(bf16[2,4,1,6,960]{4,1,3,2,0:T(4,128)(2,1)} %copy.68), calls=%async_computation | async-start | bytes 196608 | tf_op jit(solution)/shard_map/all_to_all | solution.py:34
  12.0 10.1 %all-to-all-start.1 = ((bf16[2,4,1,6,960]{4,0,3,2,1:T(2,128)(2,1)}), bf16[2,4,1,6,960]{4,0,3,2,1:T(2,128)(2,1)S(1)}, u32[]{:S(2)}, u32[]{:S(2)}) async-start(bf16[2,4,1,6,960]{4,0,3,2,1:T(2,128)(2,1)} %copy.69), calls=%async_computation.1 | async-start | bytes 196608 | tf_op jit(solution)/shard_map/all_to_all | solution.py:34
  55.5 2.5 %copy-start.6 = (f32[512]{0:T(512)S(1)}, f32[512]{0:T(512)}, u32[]{:S(2)}) copy-start(f32[512]{0:T(512)} %param.21) | copy-start | bytes 6148
  59.0 15.6 %collective-permute-start.1 = (bf16[3,3,12,512]{3,2,1,0:T(8,128)(2,1)}, bf16[3,3,12,512]{3,2,1,0:T(8,128)(2,1)}, u32[]{:S(2)}, u32[]{:S(2)}) collective-permute-start(bf16[3,3,12,512]{3,2,1,0:T(8,128)(2,1)} %get-tuple-element.10), channel_id=1, source_target_pairs={{2,0},{4,2},{6,4},{8,6},{10,8},{12,10},{14,12},{16,14},{18,16},{20... | collective-permute-start | bytes 331784 | tf_op jit(solution)/shard_map/ppermute | solution.py:51
  62.2 12.3 %collective-permute-start = (bf16[3,3,12,512]{3,2,1,0:T(8,128)(2,1)}, bf16[3,3,12,512]{3,2,1,0:T(8,128)(2,1)}, u32[]{:S(2)}, u32[]{:S(2)}) collective-permute-start(bf16[3,3,12,512]{3,2,1,0:T(8,128)(2,1)} %get-tuple-element.9), channel_id=1, source_target_pairs={{0,2},{2,4},{4,6},{6,8},{8,10},{10,12},{12,14},{14,16},{16,18},{18... | collective-permute-start | bytes 331784 | tf_op jit(solution)/shard_map/ppermute | solution.py:48
  84.3 3.2 %copy-start.3 = (bf16[3,12,12,512]{3,2,1,0:T(8,128)(2,1)S(1)}, bf16[3,12,12,512]{3,2,1,0:T(8,128)(2,1)}, u32[]{:S(2)}) copy-start(bf16[3,12,12,512]{3,2,1,0:T(8,128)(2,1)} %get-tuple-element.7) | copy-start | bytes 1327108
  89.4 2.1 %copy-start.1 = (bf16[2,1,3,6,12,16,32]{6,5,4,3,2,0,1:T(8,128)(2,1)S(1)}, bf16[2,1,3,6,12,16,32]{6,5,4,3,2,0,1:T(8,128)(2,1)}, u32[]{:S(2)}) copy-start(bf16[2,1,3,6,12,16,32]{6,5,4,3,2,0,1:T(8,128)(2,1)} %copy.78) | copy-start | bytes 1327108
  89.4 2.5 %copy-start.2 = (bf16[2,1,3,6,12,16,32]{6,5,4,3,2,0,1:T(8,128)(2,1)S(1)}, bf16[2,1,3,6,12,16,32]{6,5,4,3,2,0,1:T(8,128)(2,1)}, u32[]{:S(2)}) copy-start(bf16[2,1,3,6,12,16,32]{6,5,4,3,2,0,1:T(8,128)(2,1)} %copy.79) | copy-start | bytes 1327108
  99.4 3.4 %copy-start.4 = (f32[216,512]{1,0:T(8,128)S(1)}, f32[216,512]{1,0:T(8,128)}, u32[]{:S(2)}) copy-start(f32[216,512]{1,0:T(8,128)} %reshape.137) | copy-start | bytes 1327108
  102.8 1.8 %copy-start.7 = (f32[512]{0:T(512)S(1)}, f32[512]{0:T(512)}, u32[]{:S(2)}) copy-start(f32[512]{0:T(512)} %param.25) | copy-start | bytes 6148
where the time goes:
time: 109 us; the launch traced here: 108 us
  local copies, waits for them, and re-layouts  42.9 us (39%)
  matrix products  32.1 us (29%)
  starting transfers between devices  15.8 us (14%)
  waiting for transfers between devices  9.25 us (8%)
  other arithmetic  7.95 us (7%)
    all_to_all x2, waiting for transfers between devices, moved_by_axis(): lax.all_to_all(parts, axes[k], split_axis=k, concat_axis=k, tiled=True)  9.25 us
    dot_general x1, matrix products, level_partials(): jnp.einsum('lrwhc,qhc->qrwhl', key_rows, queries, preferred_element_type=...  9.15 us
    transpose x3, local copies, waits for them, and re-layouts, windows_of(): blocks = blocks.transpose(1, 3, 0, 2, 4, 5, 6)  8.38 us
    all_to_all x2, starting transfers between devices, moved_by_axis(): lax.all_to_all(parts, axes[k], split_axis=k, concat_axis=k, tiled=True)  7.85 us
    dot_general x1, matrix products, level_partials(): jnp.einsum('qrwhl,lrwhc->qrwhc', weights, value_rows.astype(jnp.float32),...  7.69 us
    reshape x3, local copies, waits for them, and re-layouts, windows_of(): tensor.reshape(level_count, row_count // WLAT, WLAT, col_count // WLON, W...  7.47 us
    exp x1, local copies, waits for them, and re-layouts, level_partials(): weights = jnp.exp(scores - maxima[..., None])  5.31 us
    ppermute x1, starting transfers between devices, with_halo(): lax.ppermute(lax.slice_in_dim(block, block.shape[dim] - width, None, axis...  4.7 us
  transfers between devices with their start and end apart: 4, of which 2 were waited for; matrix products, arithmetic and copies ran while one was open for 9% of the time, Pallas kernels for 0%

commit v1 on v0

v1 whole, which is shorter than its diff:
```python
import functools

import jax
import jax.numpy as jnp
from jax import lax
from jax.experimental import pallas as pl
from jax.experimental.pallas import tpu as pltpu
from jax.sharding import PartitionSpec as P

HEADS = 16
HEAD = 32
D = 512
LATENT = 3
LEVELS = 8
ROWS = 6
COLS = 12
PIXELS = 80
SHIFT = 3
WIDE = 1024
HALF = 112
FILLED = 108
TOKENS = 2 * HALF
FOLDED = 768
EPSILON = 1e-05
MASKED = -1e30
SCALE = HEAD**-0.5
F32 = jnp.float32
BF16 = jnp.bfloat16


def dot(a, b):
    return jnp.dot(a, b, preferred_element_type=F32)


def dot_nt(a, b):
    return lax.dot_general(a, b, (((1,), (1,)), ((), ())), preferred_element_type=F32)


def split(a):
    high = a.astype(BF16)
    return high, (a - high.astype(F32)).astype(BF16)


def iota(shape, dim):
    return lax.broadcasted_iota(jnp.int32, shape, dim)


def layer_norm(tensor, scales):
    center = jnp.mean(tensor, axis=-1, keepdims=True)
    offset = tensor - center
    spread = jnp.mean(offset * offset, axis=-1, keepdims=True)
    return offset * lax.rsqrt(spread + EPSILON) * scales


def blocks_kernel(pixels, out):
    out[...] = jnp.zeros_like(out)
    wide = pixels[0].astype(F32)
    for v in range(8):
        out[v, :ROWS, : COLS * PIXELS] = wide[:, v * COLS * PIXELS : (v + 1) * COLS * PIXELS].astype(BF16)


def fold_kernel(bias, embed, query, key, value, folded, folded_bias):
    head_of_lane = iota((HEADS, D), 1) // HEAD
    own = head_of_lane == iota((HEADS, D), 0)
    spread = [jnp.where(own, query[q : q + 1].astype(F32), 0.0) for q in range(LATENT)]
    spread.append(jnp.zeros((128 - LATENT * HEADS, D), F32))
    spread = jnp.concatenate(spread, axis=0).astype(BF16)
    high, low = split(dot_nt(key[...], spread))
    scores = dot(embed[...], high) + dot(embed[...], low)
    high_score, low_score = split(scores)
    values = dot(embed[...], value[...]).astype(BF16)
    whole = jnp.concatenate([values, high_score, low_score], axis=1)
    folded[...] = jnp.zeros_like(folded)
    for k in range(8):
        folded[k, 16 * k : 16 * k + PIXELS] = whole
    folded_bias[:, :D] = dot(bias[...], value[...])
    folded_bias[:, D:] = dot(bias[...], high) + dot(bias[...], low)


def pool_rows(x, folded, folded_bias, values, weights, pooled):
    bias_value = folded_bias[:, :D][:, None, :]
    bias_score = folded_bias[:, D:][:, None, :]
    for j in range(COLS):
        start, offset = j * PIXELS // 128 * 128, j * PIXELS % 128
        got = dot(x[:, start : start + 256], folded[offset // 16])
        values[j] = got[:, :D].reshape(LEVELS, 8, D) + bias_value
        score = (got[:, D : D + 128] + got[:, D + 128 :]).reshape(LEVELS, 8, 128) + bias_score
        share = jnp.exp((score - jnp.max(score, axis=0, keepdims=True)) * SCALE)
        share = share / jnp.sum(share, axis=0, keepdims=True)
        high, low = split(share.reshape(64, 128))
        weights[j * 64 : (j + 1) * 64, :128] = high
        weights[j * 64 : (j + 1) * 64, 128:] = low
    for q in range(LATENT):
        lane = (iota((256, D), 1) >> 5) + q * HEADS
        expand = jnp.where((iota((256, D), 0) & 127) == lane, 1.0, 0.0).astype(BF16)
        full = dot(weights[...], expand).reshape(COLS, LEVELS, 8, D)
        total = jnp.sum(full * values[...], axis=1)
        pooled[q * 96 : (q + 1) * 96] = total.reshape(96, D).astype(BF16)
    source = iota((1, 288), 1)
    q = (source >= 96).astype(jnp.int32) + (source >= 192).astype(jnp.int32)
    j = (source - 96 * q) >> 3
    row = source & 7
    half = (row >= 3).astype(jnp.int32)
    target = half * HALF + (q * 3 + row - 3 * half) * 12 + j
    target = jnp.where(row < ROWS, target, -1)
    pick = jnp.where(iota((TOKENS, 288), 0) == target, 1.0, 0.0).astype(BF16)
    return dot(pick, pooled[...]).astype(BF16)


def latent_rows(pooled, query, output):
    place = iota((TOKENS, 1), 0)
    place = jnp.where(place >= HALF, place - HALF, place)
    first, second, third = (query[q : q + 1].astype(F32) for q in range(LATENT))
    added = jnp.where(place < 36, first, jnp.where(place < 72, second, third))
    return (dot(pooled, output[...]) + added).astype(BF16)


def own_kernel(x, folded, folded_bias, query, output, gain, to_query, to_context,
               latent, spread_query, context, values, weights, pooled):
    rows = pool_rows(x[...].reshape(64, WIDE), folded, folded_bias, values, weights, pooled)
    tokens = latent_rows(rows, query, output)
    latent[...] = tokens
    normed = layer_norm(tokens.astype(F32), gain[...]).astype(BF16)
    queries = dot(normed, to_query[...]).astype(BF16).astype(F32)
    context[...] = dot(normed, to_context[...]).astype(BF16)
    spread_query[...] = jnp.zeros_like(spread_query)
    for half in range(2):
        part = queries[half * HALF : (half + 1) * HALF]
        part = jnp.concatenate([part, jnp.zeros((128 - HALF, D), F32)], axis=0)
        turned = part.T.astype(BF16)
        for head in range(HEADS):
            group, place = divmod(head, 8)
            spread_query[half * 2 + group, place * HEAD : (place + 1) * HEAD, place * 128 : (place + 1) * 128] = (
                turned[head * HEAD : (head + 1) * HEAD]
            )


def block_kernel(bands, x, folded, folded_bias, query, output, gain, to_context, latent, spread_query, context,
                 mix, second_gain, up, down, out, values, weights, pooled):
    rows = pool_rows(x[...].reshape(64, WIDE), folded, folded_bias, values, weights, pooled)
    tokens = latent_rows(rows, query, output)
    normed = layer_norm(tokens.astype(F32), gain[...]).astype(BF16)
    beside = dot(normed, to_context[...]).astype(BF16)
    band = lax.axis_index("lat")
    place = iota((TOKENS, 1), 0)
    filled = jnp.where(place >= HALF, place - HALF, place) < FILLED
    mixed = []
    for half in range(2):
        own = context[half * HALF : (half + 1) * HALF]
        near = jnp.concatenate([own, beside[half * HALF : (half + 1) * HALF]], axis=0)
        there = band > 0 if half == 0 else band < bands - 1
        usable = filled & ((place < HALF) | there)
        mask = jnp.where(usable, 0.0, MASKED)
        parts = []
        for group in range(2):
            keys = near[:, group * 256 : (group + 1) * 256]
            score = dot(keys, spread_query[half * 2 + group]) + mask
            share = jnp.exp((score - jnp.max(score, axis=0, keepdims=True)) * SCALE)
            inverse = 1.0 / jnp.sum(share, axis=0, keepdims=True)
            share = share.astype(BF16)
            turned = near[:, D + group * 256 : D + (group + 1) * 256].astype(F32).T.astype(BF16)
            for head in range(8):
                lanes = slice(head * 128, (head + 1) * 128)
                part = dot(turned[head * HEAD : (head + 1) * HEAD], share[:, lanes])
                parts.append(part * inverse[:, lanes])
        attended = jnp.concatenate(parts, axis=0).T.astype(BF16)
        mixed.append(dot(attended, mix[...])[:HALF])
    mixed = jnp.concatenate(mixed, axis=0) + latent[...].astype(F32)
    second = layer_norm(mixed, second_gain[...]).astype(BF16)
    hidden = jax.nn.gelu(dot(second, up[...])).astype(BF16)
    result = mixed + dot(hidden, down[...])
    for half in range(2):
        for q in range(LATENT):
            for i in range(3):
                start = half * HALF + (q * 3 + i) * COLS
                out[q, half * 3 + i] = result[start : start + COLS].astype(BF16)


def call(kernel, outs, scratch=(), flops=0, moved=0, limit=32):
    return pl.pallas_call(
        kernel,
        out_shape=outs,
        scratch_shapes=list(scratch),
        compiler_params=pltpu.CompilerParams(vmem_limit_bytes=limit * 2**20),
        cost_estimate=pl.CostEstimate(flops=flops, bytes_accessed=moved, transcendentals=0),
    )


def shaped(*shape, dtype=BF16):
    return jax.ShapeDtypeStruct(shape, dtype)


def body(
    patches,
    level_bias,
    embed_weight,
    latent_query,
    cross_key,
    cross_value,
    cross_output,
    first_gain,
    window_query,
    window_context,
    window_output,
    second_gain,
    up_weight,
    down_weight,
):
    bands = lax.axis_size("lat")
    blocks = call(blocks_kernel, shaped(8, 8, WIDE), flops=10**6, moved=10**6)(patches)
    x = lax.all_to_all(blocks, "var", 0, 0, tiled=True)
    folded, folded_bias = call(
        fold_kernel,
        (shaped(8, 256, FOLDED), shaped(LEVELS, D + 128, dtype=F32)),
        flops=10**9,
        moved=6 * 10**6,
    )(level_bias, embed_weight, latent_query, cross_key, cross_value)
    forward = [(i, i + 1) for i in range(bands - 1)]
    backward = [(i + 1, i) for i in range(bands - 1)]
    low = lax.ppermute(x[:, SHIFT:ROWS], "lat", forward)
    high = lax.ppermute(x[:, :SHIFT], "lat", backward)
    scratch = (
        pltpu.VMEM((COLS, LEVELS, 8, D), F32),
        pltpu.VMEM((COLS * 64, 256), BF16),
        pltpu.VMEM((LATENT * 96, D), BF16),
    )
    gain = first_gain.reshape(1, D)
    latent, spread_query, context = call(
        own_kernel,
        (shaped(TOKENS, D), shaped(4, 256, 1024), shaped(TOKENS, 2 * D)),
        scratch,
        flops=3 * 10**9,
        moved=10**7,
    )(x, folded, folded_bias, latent_query, cross_output, gain, window_query, window_context)
    beside = jnp.concatenate([low, high, jnp.zeros((LEVELS, 2, WIDE), BF16)], axis=1)
    return call(
        functools.partial(block_kernel, bands),
        shaped(LATENT, ROWS, COLS, D),
        scratch,
        flops=4 * 10**9,
        moved=10**7,
    )(beside, folded, folded_bias, latent_query, cross_output, gain, window_context, latent, spread_query, context,
      window_output, second_gain.reshape(1, D), up_weight, down_weight)


def solution(mesh):
    return jax.shard_map(
        body,
        mesh=mesh,
        in_specs=(P(("dp", "var"), "lat", None),) + (P(),) * 13,
        out_specs=P("dp", "lat", "var", None),
        check_vma=False,
    )
```

time: 109 us -> 37.8 us (0.35)
  local copies, waits for them, and re-layouts: 42.9 us -> 8.94 us
  matrix products: 32.1 us -> 0 us
  Pallas kernels: 0 us -> 11.6 us
  other arithmetic: 7.95 us -> 0.09 us
  waiting for transfers between devices: 9.25 us -> 2.64 us
  starting transfers between devices: 15.8 us -> 13.9 us
    dot_general x12 -> x0, matrix products: 32.1 us -> none  [the longest x1 9.15 us: level_partials(): jnp.einsum('lrwhc,qhc->qrwhl', key_rows, queries, preferred_element_type=...]
    reshape x16 -> x0, local copies, waits for them, and re-layouts: 20.5 us -> none  [the longest x3 7.47 us: windows_of(): tensor.reshape(level_count, row_count // WLAT, WLAT, col_count // WLON, W...]
    pallas_call x0 -> x4, Pallas kernels: none -> 11.6 us  [the longest x1 7.16 us: body(): call(functools.partial(block_kernel, bands), shaped(LATENT, ROWS, COLS, D...]
    transpose x4 -> x0, local copies, waits for them, and re-layouts: 8.47 us -> none  [the longest x3 8.38 us: windows_of(): blocks = blocks.transpose(1, 3, 0, 2, 4, 5, 6)]
    unnamed x16 -> x34, local copies, waits for them, and re-layouts: 0.49 us -> 8.82 us
    all_to_all x2 -> x1, waiting for transfers between devices: 9.25 us -> 1.09 us  [body(): x = lax.all_to_all(blocks, 'var', 0, 0, tiled=True)]
    exp x1 -> x0, local copies, waits for them, and re-layouts: 5.31 us -> none  [level_partials(): weights = jnp.exp(scores - maxima[..., None])]
    convert_element_type x3 -> x0, local copies, waits for them, and re-layouts: 3.37 us -> none  [the longest x1 2.42 us: window_attend(): attended = jnp.einsum('bhts,bshc->bthc', shares, value_rows, preferred_el...]
  transfers between devices with their start and end apart: 4 -> 3, of which waited for: 2 -> 2; matrix products, arithmetic and copies ran while one was open for 9% -> 0% of each run, Pallas kernels for 0% -> 10%
where the time goes in v1:
time: 37.8 us; the launch traced here: 37.3 us
  starting transfers between devices  13.9 us (37%)
  Pallas kernels  11.6 us (31%)
  local copies, waits for them, and re-layouts  8.94 us (24%)
  waiting for transfers between devices  2.64 us (7%)
    unnamed x34, local copies, waits for them, and re-layouts  8.82 us
    pallas_call x1, Pallas kernels, body(): call(functools.partial(block_kernel, bands), shaped(LATENT, ROWS, COLS, D...  7.16 us
    all_to_all x1, starting transfers between devices, body(): x = lax.all_to_all(blocks, 'var', 0, 0, tiled=True)  6.16 us
    ppermute x1, starting transfers between devices, body(): low = lax.ppermute(x[:, SHIFT:ROWS], 'lat', forward)  5.82 us
    pallas_call x1, Pallas kernels, body(): call(own_kernel, (shaped(TOKENS, D), shaped(4, 256, 1024), shaped(TOKENS,...  2.83 us
    ppermute x1, starting transfers between devices, body(): high = lax.ppermute(x[:, :SHIFT], 'lat', backward)  1.92 us
    ppermute x1, waiting for transfers between devices, body(): high = lax.ppermute(x[:, :SHIFT], 'lat', backward)  1.54 us
    all_to_all x1, waiting for transfers between devices, body(): x = lax.all_to_all(blocks, 'var', 0, 0, tiled=True)  1.09 us
  transfers between devices with their start and end apart: 3, of which 2 were waited for; matrix products, arithmetic and copies ran while one was open for 0% of the time, Pallas kernels for 10%

profile of v1, /device:TPU:104, one launch (start us, length us, event | category | flops | bytes accessed | tf_op | source)
XLA Modules:
  0.0 37.3 jit_solution(3928859242015804218)
XLA Ops:
  0.0 0.0 copy-start
  0.0 0.9 %copy-done = bf16[1,6,7680]{2,1,0:T(8,128)(2,1)S(1)} copy-done((bf16[1,6,7680]{2,1,0:T(8,128)(2,1)S(1)}, bf16[1,6,7680]{2,1,0:T(8,128)(2,1)}, u32[]{:S(2)}) %copy-start) | copy-done | bytes 92184
  0.9 0.0 copy-start.12
  0.9 0.0 copy-start.13
  0.9 0.7 %shard_map.136 = bf16[8,8,1024]{2,1,0:T(8,128)(2,1)} custom-call(bf16[1,6,7680]{2,1,0:T(8,128)(2,1)S(1)} %copy-done), custom_call_target="tpu_custom_call" | custom-call | flops 1000000 | bytes 1000000 | tf_op jit(solution)/shard_map/pallas_call | solution.py:210
  1.7 0.0 copy-start.3
  1.7 6.2 %all-to-all-start = ((bf16[8,8,1024]{2,1,0:T(8,128)(2,1)}), bf16[8,8,1024]{2,1,0:T(8,128)(2,1)S(1)}, u32[]{:S(2)}, u32[]{:S(2)}) async-start(bf16[8,8,1024]{2,1,0:T(8,128)(2,1)} %shard_map.136), calls=%async_computation | async-start | bytes 262144 | tf_op jit(solution)/shard_map/all_to_all | solution.py:211
  7.8 0.1 pad.2.clone
  7.9 0.0 copy-start.4
  7.9 1.0 %copy-done.4 = bf16[512,512]{1,0:T(8,128)(2,1)S(1)} copy-done((bf16[512,512]{1,0:T(8,128)(2,1)S(1)}, bf16[512,512]{1,0:T(8,128)(2,1)}, u32[]{:S(2)}) %copy-start.4) | copy-done | bytes 524312
  8.9 0.0 copy-start.5
  8.9 1.0 %copy-done.5 = bf16[512,512]{1,0:T(8,128)(2,1)S(1)} copy-done((bf16[512,512]{1,0:T(8,128)(2,1)S(1)}, bf16[512,512]{1,0:T(8,128)(2,1)}, u32[]{:S(2)}) %copy-start.5) | copy-done | bytes 524312
  10.0 0.0 copy-start.9
  10.0 0.9 %copy-done.9 = bf16[80,512]{1,0:T(8,128)(2,1)S(1)} copy-done((bf16[80,512]{1,0:T(8,128)(2,1)S(1)}, bf16[80,512]{1,0:T(8,128)(2,1)}, u32[]{:S(2)}) %copy-start.9) | copy-done | bytes 81944
  10.9 0.0 copy-start.10
  10.9 0.7 %copy-done.10 = bf16[8,512]{1,0:T(8,128)(2,1)S(1)} copy-done((bf16[8,512]{1,0:T(8,128)(2,1)S(1)}, bf16[8,512]{1,0:T(8,128)(2,1)}, u32[]{:S(2)}) %copy-start.10) | copy-done | bytes 8216
  11.6 0.0 copy-start.11
  11.6 0.7 %copy-done.11 = bf16[3,512]{1,0:T(4,128)(2,1)S(1)} copy-done((bf16[3,512]{1,0:T(4,128)(2,1)S(1)}, bf16[3,512]{1,0:T(4,128)(2,1)}, u32[]{:S(2)}) %copy-start.11) | copy-done | bytes 3096
  12.3 0.0 copy-start.6
  12.3 0.0 copy-start.7
  12.3 0.9 %shard_map.137 = (bf16[8,256,768]{2,1,0:T(8,128)(2,1)S(1)}, f32[8,640]{1,0:T(8,128)S(1)}) custom-call(bf16[8,512]{1,0:T(8,128)(2,1)S(1)} %copy-done.10, bf16[80,512]{1,0:T(8,128)(2,1)S(1)} %copy-done.9, bf16[3,512]{1,0:T(4,128)(2,1)S(1)} %copy-done.11, bf16[512,512]{1,0:T(8,128)(2,1)S(1)} %copy-done.4, bf16[512,512]{1,0:T(8,128)(2,1)S(1)} %copy-done.5), custom_call_target="tpu_custom_call" | custom-call | flops 1000000000 | bytes 6000000 | tf_op jit(solution)/shard_map/pallas_call | solution.py:212
  13.2 0.0 copy-start.15
  13.2 1.6 %copy-done.15 = bf16[8,256,768]{2,1,0:T(8,128)(2,1)} copy-done((bf16[8,256,768]{2,1,0:T(8,128)(2,1)}, bf16[8,256,768]{2,1,0:T(8,128)(2,1)S(1)}, u32[]{:S(2)}) %copy-start.15) | copy-done | bytes 3145752
  14.8 1.1 %all-to-all-done.x = bf16[8,8,1024]{2,1,0:T(8,128)(2,1)S(1)} async-done(((bf16[8,8,1024]{2,1,0:T(8,128)(2,1)}), bf16[8,8,1024]{2,1,0:T(8,128)(2,1)S(1)}, u32[]{:S(2)}, u32[]{:S(2)}) %all-to-all-start) | async-done | bytes 131104 | tf_op jit(solution)/shard_map/all_to_all | solution.py:211
  16.0 5.8 %collective-permute-start = (bf16[8,3,1024]{2,1,0:T(4,128)(2,1)S(1)}, bf16[8,3,1024]{2,1,0:T(4,128)(2,1)S(1)}, u32[]{:S(2)}, u32[]{:S(2)}) collective-permute-start(bf16[8,3,1024]{2,1,0:T(4,128)(2,1)S(1)} %get-tuple-element.15), channel_id=1, source_target_pairs={{0,2},{2,4},{4,6},{6,8},{8,10},{10,12},{12,14},{14,16},{16,18},{18... | collective-permute-start | bytes 147464 | tf_op jit(solution)/shard_map/ppermute | solution.py:220
  21.8 1.9 %collective-permute-start.1 = (bf16[8,3,1024]{2,1,0:T(4,128)(2,1)S(1)}, bf16[8,3,1024]{2,1,0:T(4,128)(2,1)S(1)}, u32[]{:S(2)}, u32[]{:S(2)}) collective-permute-start(bf16[8,3,1024]{2,1,0:T(4,128)(2,1)S(1)} %get-tuple-element.16), channel_id=1, source_target_pairs={{2,0},{4,2},{6,4},{8,6},{10,8},{12,10},{14,12},{16,14},{18,16},{20... | collective-permute-start | bytes 147464 | tf_op jit(solution)/shard_map/ppermute | solution.py:221
  23.7 0.0 copy-done.12
  23.7 0.0 copy-done.13
  23.7 0.0 copy-done.3
  23.7 0.0 copy-done.6
  23.8 0.0 copy-done.7
  23.8 0.0 copy-start.16
  23.8 1.9 %copy-done.16 = bf16[8,256,768]{2,1,0:T(8,128)(2,1)S(1)} copy-done((bf16[8,256,768]{2,1,0:T(8,128)(2,1)S(1)}, bf16[8,256,768]{2,1,0:T(8,128)(2,1)}, u32[]{:S(2)}) %copy-start.16) | copy-done | bytes 3145752
  25.7 0.0 copy-start.1
  25.7 0.0 copy-start.2
  25.7 0.0 copy-start.8
  25.7 0.0 copy-start.14
  25.7 2.8 %shard_map.138 = (bf16[224,512]{1,0:T(8,128)(2,1)S(1)}, bf16[4,256,1024]{2,1,0:T(8,128)(2,1)S(1)}, bf16[224,1024]{1,0:T(8,128)(2,1)S(1)}) custom-call(bf16[8,8,1024]{2,1,0:T(8,128)(2,1)S(1)} %all-to-all-done.x, bf16[8,256,768]{2,1,0:T(8,128)(2,1)S(1)} %copy-done.16, f32[8,640]{1,0:T(8,128)S(1)} %get-tuple-element.11.folded_bias, ...), custom_call_target="tpu_custom_call" | custom-call | flops 3000000000 | bytes 10000000 | tf_op jit(solution)/shard_map/pallas_call | solution.py:228
  28.5 0.0 collective-permute-done
  28.5 1.5 %collective-permute-done.1 = bf16[8,3,1024]{2,1,0:T(4,128)(2,1)S(1)} collective-permute-done((bf16[8,3,1024]{2,1,0:T(4,128)(2,1)S(1)}, bf16[8,3,1024]{2,1,0:T(4,128)(2,1)S(1)}, u32[]{:S(2)}, u32[]{:S(2)}) %collective-permute-start.1) | collective-permute-done | bytes 49184 | tf_op jit(solution)/shard_map/ppermute | solution.py:221
  30.1 0.1 maximum_maximum_fusion.x
  30.1 0.0 copy-done.1
  30.2 0.0 copy-done.2
  30.2 0.0 copy-done.8
  30.2 0.0 copy-done.14
  30.2 7.2 %shard_map.139 = bf16[3,6,12,512]{3,2,1,0:T(8,128)(2,1)} custom-call(bf16[8,8,1024]{2,1,0:T(8,128)(2,1)S(1)} %maximum_maximum_fusion.x, bf16[8,256,768]{2,1,0:T(8,128)(2,1)S(1)} %copy-done.16, f32[8,640]{1,0:T(8,128)S(1)} %get-tuple-element.11.folded_bias, bf16[3,512]{1,0:T(4,128)(2,1)S(1)} %copy-done.12, bf16[512,512]{1,0:T(8,128)(2,1)S(1)} %copy-done.7, ...), custom_call_target="tpu_custom_call" | custom-call | flops 4000000000 | bytes 10000000 | tf_op jit(solution)/shard_map/pallas_call | solution.py:236
  (2 shorter events, 0.0 us)
Async XLA Ops:
  0.0 0.9 %copy-start = (bf16[1,6,7680]{2,1,0:T(8,128)(2,1)S(1)}, bf16[1,6,7680]{2,1,0:T(8,128)(2,1)}, u32[]{:S(2)}) copy-start(bf16[1,6,7680]{2,1,0:T(8,128)(2,1)} %pixels.1) | copy-start | bytes 276484
  0.9 22.8 %copy-start.12 = (bf16[3,512]{1,0:T(4,128)(2,1)S(1)}, bf16[3,512]{1,0:T(4,128)(2,1)}, u32[]{:S(2)}) copy-start(bf16[3,512]{1,0:T(4,128)(2,1)} %query.5) | copy-start | bytes 9220
  0.9 22.8 %copy-start.13 = (f32[512]{0:T(512)S(1)}, f32[512]{0:T(512)}, u32[]{:S(2)}) copy-start(f32[512]{0:T(512)} %param.21) | copy-start | bytes 6148
  1.7 22.1 %copy-start.3 = (bf16[512,1024]{1,0:T(8,128)(2,1)S(1)}, bf16[512,1024]{1,0:T(8,128)(2,1)}, u32[]{:S(2)}) copy-start(bf16[512,1024]{1,0:T(8,128)(2,1)} %to_context.3) | copy-start | bytes 3145732
  1.7 14.3 %all-to-all-start = ((bf16[8,8,1024]{2,1,0:T(8,128)(2,1)}), bf16[8,8,1024]{2,1,0:T(8,128)(2,1)S(1)}, u32[]{:S(2)}, u32[]{:S(2)}) async-start(bf16[8,8,1024]{2,1,0:T(8,128)(2,1)} %shard_map.136), calls=%async_computation | async-start | bytes 262144 | tf_op jit(solution)/shard_map/all_to_all | solution.py:211
  7.9 1.0 %copy-start.4 = (bf16[512,512]{1,0:T(8,128)(2,1)S(1)}, bf16[512,512]{1,0:T(8,128)(2,1)}, u32[]{:S(2)}) copy-start(bf16[512,512]{1,0:T(8,128)(2,1)} %key.1) | copy-start | bytes 1572868
  8.9 1.0 %copy-start.5 = (bf16[512,512]{1,0:T(8,128)(2,1)S(1)}, bf16[512,512]{1,0:T(8,128)(2,1)}, u32[]{:S(2)}) copy-start(bf16[512,512]{1,0:T(8,128)(2,1)} %value.1) | copy-start | bytes 1572868
  10.0 0.9 %copy-start.9 = (bf16[80,512]{1,0:T(8,128)(2,1)S(1)}, bf16[80,512]{1,0:T(8,128)(2,1)}, u32[]{:S(2)}) copy-start(bf16[80,512]{1,0:T(8,128)(2,1)} %embed.1) | copy-start | bytes 245764
  10.9 0.7 %copy-start.10 = (bf16[8,512]{1,0:T(8,128)(2,1)S(1)}, bf16[8,512]{1,0:T(8,128)(2,1)}, u32[]{:S(2)}) copy-start(bf16[8,512]{1,0:T(8,128)(2,1)} %bias.1) | copy-start | bytes 24580
  11.6 0.7 %copy-start.11 = (bf16[3,512]{1,0:T(4,128)(2,1)S(1)}, bf16[3,512]{1,0:T(4,128)(2,1)}, u32[]{:S(2)}) copy-start(bf16[3,512]{1,0:T(4,128)(2,1)} %query.5) | copy-start | bytes 9220
  12.3 11.5 %copy-start.6 = (bf16[512,512]{1,0:T(8,128)(2,1)S(1)}, bf16[512,512]{1,0:T(8,128)(2,1)}, u32[]{:S(2)}) copy-start(bf16[512,512]{1,0:T(8,128)(2,1)} %to_query.1) | copy-start | bytes 1572868
  12.3 11.5 %copy-start.7 = (bf16[512,512]{1,0:T(8,128)(2,1)S(1)}, bf16[512,512]{1,0:T(8,128)(2,1)}, u32[]{:S(2)}) copy-start(bf16[512,512]{1,0:T(8,128)(2,1)} %output.3) | copy-start | bytes 1572868
  13.2 1.7 %copy-start.15 = (bf16[8,256,768]{2,1,0:T(8,128)(2,1)}, bf16[8,256,768]{2,1,0:T(8,128)(2,1)S(1)}, u32[]{:S(2)}) copy-start(bf16[8,256,768]{2,1,0:T(8,128)(2,1)S(1)} %get-tuple-element.10.folded) | copy-start | bytes 9437188
  16.0 12.5 %collective-permute-start = (bf16[8,3,1024]{2,1,0:T(4,128)(2,1)S(1)}, bf16[8,3,1024]{2,1,0:T(4,128)(2,1)S(1)}, u32[]{:S(2)}, u32[]{:S(2)}) collective-permute-start(bf16[8,3,1024]{2,1,0:T(4,128)(2,1)S(1)} %get-tuple-element.15), channel_id=1, source_target_pairs={{0,2},{2,4},{4,6},{6,8},{8,10},{10,12},{12,14},{14,16},{16,18},{18... | collective-permute-start | bytes 147464 | tf_op jit(solution)/shard_map/ppermute | solution.py:220
  21.8 8.3 %collective-permute-start.1 = (bf16[8,3,1024]{2,1,0:T(4,128)(2,1)S(1)}, bf16[8,3,1024]{2,1,0:T(4,128)(2,1)S(1)}, u32[]{:S(2)}, u32[]{:S(2)}) collective-permute-start(bf16[8,3,1024]{2,1,0:T(4,128)(2,1)S(1)} %get-tuple-element.16), channel_id=1, source_target_pairs={{2,0},{4,2},{6,4},{8,6},{10,8},{12,10},{14,12},{16,14},{18,16},{20... | collective-permute-start | bytes 147464 | tf_op jit(solution)/shard_map/ppermute | solution.py:221
  23.8 1.9 %copy-start.16 = (bf16[8,256,768]{2,1,0:T(8,128)(2,1)S(1)}, bf16[8,256,768]{2,1,0:T(8,128)(2,1)}, u32[]{:S(2)}) copy-start(bf16[8,256,768]{2,1,0:T(8,128)(2,1)} %copy-done.15) | copy-start | bytes 9437188
  25.7 4.5 %copy-start.1 = (bf16[512,2048]{1,0:T(8,128)(2,1)S(1)}, bf16[512,2048]{1,0:T(8,128)(2,1)}, u32[]{:S(2)}) copy-start(bf16[512,2048]{1,0:T(8,128)(2,1)} %up.1) | copy-start | bytes 6291460
  25.7 4.5 %copy-start.2 = (bf16[2048,512]{1,0:T(8,128)(2,1)S(1)}, bf16[2048,512]{1,0:T(8,128)(2,1)}, u32[]{:S(2)}) copy-start(bf16[2048,512]{1,0:T(8,128)(2,1)} %down.1) | copy-start | bytes 6291460
  25.7 4.5 %copy-start.8 = (bf16[512,512]{1,0:T(8,128)(2,1)S(1)}, bf16[512,512]{1,0:T(8,128)(2,1)}, u32[]{:S(2)}) copy-start(bf16[512,512]{1,0:T(8,128)(2,1)} %mix.1) | copy-start | bytes 1572868
  25.7 4.5 %copy-start.14 = (f32[512]{0:T(512)S(1)}, f32[512]{0:T(512)}, u32[]{:S(2)}) copy-start(f32[512]{0:T(512)} %param.25) | copy-start | bytes 6148

commit v2 on v1

v2 whole, which is shorter than its diff:
```python
import functools

import jax
import jax.numpy as jnp
from jax import lax
from jax.experimental import pallas as pl
from jax.experimental.pallas import tpu as pltpu
from jax.sharding import Mesh
from jax.sharding import PartitionSpec as P

HEADS = 16
HEAD = 32
D = 512
LATENT = 3
LEVELS = 8
ROWS = 6
COLS = 12
PIXELS = 80
WIDE = 1024
HALF = 112
FILLED = 108
TOKENS = 2 * HALF
FOLDED = 768
EPSILON = 1e-05
MASKED = -1e30
SCALE = HEAD**-0.5
F32 = jnp.float32
BF16 = jnp.bfloat16


def dot(a, b):
    return jnp.dot(a, b, preferred_element_type=F32)


def dot_nt(a, b):
    return lax.dot_general(a, b, (((1,), (1,)), ((), ())), preferred_element_type=F32)


def split(a):
    high = a.astype(BF16)
    return high, (a - high.astype(F32)).astype(BF16)


def iota(shape, dim):
    return lax.broadcasted_iota(jnp.int32, shape, dim)


def layer_norm(tensor, scales):
    center = jnp.mean(tensor, axis=-1, keepdims=True)
    offset = tensor - center
    spread = jnp.mean(offset * offset, axis=-1, keepdims=True)
    return offset * lax.rsqrt(spread + EPSILON) * scales


def blocks_kernel(pixels, out, held, arrived):
    copy = pltpu.make_async_copy(pixels, held, arrived)
    copy.start()
    out[...] = jnp.zeros_like(out)
    copy.wait()
    wide = held[0].astype(F32)
    for v in range(LEVELS):
        block = wide[:, v * COLS * PIXELS : (v + 1) * COLS * PIXELS].astype(BF16)
        out[2 * v, :ROWS, : COLS * PIXELS] = block
        out[2 * v + 1, :ROWS, : COLS * PIXELS] = block


def pick_matrix(swapped):
    source = iota((1, 288), 1)
    q = (source >= 96).astype(jnp.int32) + (source >= 192).astype(jnp.int32)
    j = (source - 96 * q) >> 3
    row = source & 7
    lower = (row >= 3).astype(jnp.int32)
    half = 1 - lower if swapped else lower
    target = half * HALF + (q * 3 + row - 3 * lower) * COLS + j
    target = jnp.where(row < ROWS, target, -1)
    return jnp.where(iota((TOKENS, 288), 0) == target, 1.0, 0.0).astype(BF16)


def fold_kernel(bias_hbm, embed_hbm, query_hbm, key_hbm, value_hbm, folded, folded_bias, expand,
                bias, embed, query, key, value, arrived):
    pairs = ((query_hbm, query), (key_hbm, key), (embed_hbm, embed), (value_hbm, value), (bias_hbm, bias))
    copies = [pltpu.make_async_copy(*pair, arrived.at[k]) for k, pair in enumerate(pairs)]
    for copy in copies:
        copy.start()
    for q in range(LATENT):
        lane = (iota((256, D), 1) >> 5) + q * HEADS
        expand[:, q * D : (q + 1) * D] = jnp.where((iota((256, D), 0) & 127) == lane, 1.0, 0.0).astype(BF16)
    for copy in copies:
        copy.wait()
    own = iota((HEADS, D), 1) // HEAD == iota((HEADS, D), 0)
    spread = [jnp.where(own, query[q : q + 1].astype(F32), 0.0) for q in range(LATENT)]
    spread.append(jnp.zeros((128 - LATENT * HEADS, D), F32))
    spread = jnp.concatenate(spread, axis=0).astype(BF16)
    high, low = split(dot_nt(key[...], spread))
    scores = dot(embed[...], high) + dot(embed[...], low)
    high_score, low_score = split(scores)
    folded[PIXELS:] = jnp.zeros((128 - PIXELS, FOLDED), BF16)
    folded[:PIXELS, :D] = dot(embed[...], value[...]).astype(BF16)
    folded[:PIXELS, D : D + 128] = high_score
    folded[:PIXELS, D + 128 :] = low_score
    folded_bias[:, :D] = dot(bias[...], value[...])
    folded_bias[:, D:] = dot(bias[...], high) + dot(bias[...], low)


def pool_rows(x, folded, folded_bias, expand, query, output, swapped, rows, values, weights, pooled):
    for j in range(COLS):
        rows[j * 64 : (j + 1) * 64] = x[:, j * PIXELS : j * PIXELS + 128].astype(BF16)
    values[...] = dot(rows[...], folded[:, :D]).reshape(COLS, LEVELS, 8, D) + folded_bias[:, :D][None, :, None, :]
    both = dot(rows[...], folded[:, D:])
    score = (both[:, :128] + both[:, 128:]).reshape(COLS, LEVELS, 8, 128) + folded_bias[:, D:][None, :, None, :]
    share = jnp.exp((score - jnp.max(score, axis=1, keepdims=True)) * SCALE)
    share = share / jnp.sum(share, axis=1, keepdims=True)
    high, low = split(share.reshape(COLS * 64, 128))
    weights[:, :128] = high
    weights[:, 128:] = low
    for q in range(LATENT):
        full = dot(weights[...], expand[:, q * D : (q + 1) * D]).reshape(COLS, LEVELS, 8, D)
        total = jnp.sum(full * values[...], axis=1)
        pooled[q * 96 : (q + 1) * 96] = total.reshape(96, D).astype(BF16)
    picked = dot(pick_matrix(swapped), pooled[...]).astype(BF16)
    place = iota((TOKENS, 1), 0)
    place = jnp.where(place >= HALF, place - HALF, place)
    first, second, third = (query[q : q + 1].astype(F32) for q in range(LATENT))
    added = jnp.where(place < 36, first, jnp.where(place < 72, second, third))
    return (dot(picked, output[...]) + added).astype(BF16)


def own_kernel(x, folded, folded_bias, expand, query, output, gain, to_query, to_context,
               latent, spread_query, context, *scratch):
    own = x[:, pl.ds(lax.axis_index("near"), 1)].reshape(64, WIDE).astype(F32)
    tokens = pool_rows(own, folded, folded_bias, expand, query, output, False, *scratch)
    latent[...] = tokens
    normed = layer_norm(tokens.astype(F32), gain[...]).astype(BF16)
    queries = dot(normed, to_query[...]).astype(BF16).astype(F32)
    context[...] = dot(normed, to_context[...]).astype(BF16)
    spread_query[...] = jnp.zeros_like(spread_query)
    for half in range(2):
        part = queries[half * HALF : (half + 1) * HALF]
        part = jnp.concatenate([part, jnp.zeros((128 - HALF, D), F32)], axis=0)
        turned = part.T.astype(BF16)
        for head in range(HEADS):
            group, place = divmod(head, 8)
            spread_query[half * 2 + group, place * HEAD : (place + 1) * HEAD, place * 128 : (place + 1) * 128] = (
                turned[head * HEAD : (head + 1) * HEAD]
            )


def block_kernel(pairs, x, beyond, folded, folded_bias, expand, query, output, gain, to_context,
                 latent, spread_query, context, mix, second_gain, up, down, out, *scratch):
    near = lax.axis_index("near")
    inner = x[:, pl.ds(1 - near, 1)].reshape(64, WIDE).astype(F32)
    lower = (iota((64, 1), 0) & 7) >= 3
    halo = jnp.where(lower == (near == 1), inner, beyond[...].reshape(64, WIDE).astype(F32))
    tokens = pool_rows(halo, folded, folded_bias, expand, query, output, True, *scratch)
    normed = layer_norm(tokens.astype(F32), gain[...]).astype(BF16)
    beside = dot(normed, to_context[...]).astype(BF16)
    band = lax.axis_index("far") * 2 + near
    place = iota((TOKENS, 1), 0)
    filled = jnp.where(place >= HALF, place - HALF, place) < FILLED
    mixed = []
    for half in range(2):
        own = context[half * HALF : (half + 1) * HALF]
        keys = jnp.concatenate([own, beside[half * HALF : (half + 1) * HALF]], axis=0)
        there = band > 0 if half == 0 else band < 2 * pairs - 1
        usable = filled & ((place < HALF) | there)
        mask = jnp.where(usable, 0.0, MASKED)
        parts = []
        for group in range(2):
            score = dot(keys[:, group * 256 : (group + 1) * 256], spread_query[half * 2 + group]) + mask
            share = jnp.exp((score - jnp.max(score, axis=0, keepdims=True)) * SCALE)
            inverse = 1.0 / jnp.sum(share, axis=0, keepdims=True)
            share = share.astype(BF16)
            turned = keys[:, D + group * 256 : D + (group + 1) * 256].astype(F32).T.astype(BF16)
            for head in range(8):
                lanes = slice(head * 128, (head + 1) * 128)
                part = dot(turned[head * HEAD : (head + 1) * HEAD], share[:, lanes])
                parts.append(part * inverse[:, lanes])
        attended = jnp.concatenate(parts, axis=0).T.astype(BF16)
        mixed.append(dot(attended, mix[...])[:HALF])
    mixed = jnp.concatenate(mixed, axis=0) + latent[...].astype(F32)
    second = layer_norm(mixed, second_gain[...]).astype(BF16)
    hidden = jax.nn.gelu(dot(second, up[...])).astype(BF16)
    result = mixed + dot(hidden, down[...])
    for half in range(2):
        for q in range(LATENT):
            for i in range(3):
                start = half * HALF + (q * 3 + i) * COLS
                out[q, half * 3 + i] = result[start : start + COLS].astype(BF16)


def call(kernel, outs, scratch=(), flops=0, moved=0, limit=24, hbm=0):
    specs = {"in_specs": [pl.BlockSpec(memory_space=pltpu.HBM)] * hbm} if hbm else {}
    return pl.pallas_call(
        kernel,
        out_shape=outs,
        scratch_shapes=list(scratch),
        compiler_params=pltpu.CompilerParams(vmem_limit_bytes=limit * 2**20),
        cost_estimate=pl.CostEstimate(flops=flops, bytes_accessed=moved, transcendentals=0),
        **specs,
    )


def shaped(*shape, dtype=BF16):
    return jax.ShapeDtypeStruct(shape, dtype)


def body(
    patches,
    level_bias,
    embed_weight,
    latent_query,
    cross_key,
    cross_value,
    cross_output,
    first_gain,
    window_query,
    window_context,
    window_output,
    second_gain,
    up_weight,
    down_weight,
):
    pairs = lax.axis_size("far")
    blocks = call(
        blocks_kernel,
        shaped(2 * LEVELS, 8, WIDE),
        (pltpu.VMEM(patches.shape, BF16), pltpu.SemaphoreType.DMA),
        flops=10**6,
        moved=10**6,
        hbm=1,
    )(pltpu.with_memory_space_constraint(patches, pltpu.HBM))
    x = lax.all_to_all(blocks, ("var", "near"), 0, 0, tiled=True).reshape(LEVELS, 2, 8, WIDE)
    folded, folded_bias, expand = call(
        fold_kernel,
        (
            shaped(128, FOLDED),
            shaped(LEVELS, D + 128, dtype=F32),
            shaped(256, LATENT * D),
        ),
        tuple(pltpu.VMEM(a.shape, BF16) for a in (level_bias, embed_weight, latent_query, cross_key, cross_value))
        + (pltpu.SemaphoreType.DMA((5,)),),
        flops=10**9,
        moved=6 * 10**6,
        hbm=5,
    )(
        *(
            pltpu.with_memory_space_constraint(a, pltpu.HBM)
            for a in (level_bias, embed_weight, latent_query, cross_key, cross_value)
        )
    )
    swaps = [(2 * k + 1, 2 * k + 2) for k in range(pairs - 1)]
    swaps += [(b, a) for a, b in swaps]
    mine = lax.dynamic_index_in_dim(x, lax.axis_index("near"), 1, keepdims=False)
    beyond = lax.ppermute(mine, ("far", "near"), swaps)
    scratch = (
        pltpu.VMEM((COLS * 64, 128), BF16),
        pltpu.VMEM((COLS, LEVELS, 8, D), F32),
        pltpu.VMEM((COLS * 64, 256), BF16),
        pltpu.VMEM((LATENT * 96, D), BF16),
    )
    gain = first_gain.reshape(1, D)
    latent, spread_query, context = call(
        own_kernel,
        (shaped(TOKENS, D), shaped(4, 256, 1024), shaped(TOKENS, 2 * D)),
        scratch,
        flops=3 * 10**9,
        moved=10**7,
    )(x, folded, folded_bias, expand, latent_query, cross_output, gain, window_query, window_context)
    return call(
        functools.partial(block_kernel, pairs),
        shaped(LATENT, ROWS, COLS, D),
        scratch,
        flops=4 * 10**9,
        moved=10**7,
    )(x, beyond, folded, folded_bias, expand, latent_query, cross_output, gain, window_context, latent,
      spread_query, context, window_output, second_gain.reshape(1, D), up_weight, down_weight)


def solution(mesh):
    finer = Mesh(
        mesh.devices.reshape(mesh.shape["var"], mesh.shape["lat"] // 2, 2, mesh.shape["dp"]),
        ("var", "far", "near", "dp"),
    )
    return jax.shard_map(
        body,
        mesh=finer,
        in_specs=(P(("dp", "var"), ("far", "near"), None),) + (P(),) * 13,
        out_specs=P("dp", ("far", "near"), "var", None),
        check_vma=False,
    )
```

time: 37.8 us -> 33.4 us (0.88)
  the two profiles are of different devices: /device:TPU:104 before, /device:TPU:128 now
where the time goes in v2:
time: 33.4 us; the launch traced here: 33.1 us
  Pallas kernels  13.1 us (39%)
  waiting for transfers between devices  10.7 us (32%)
  starting transfers between devices  9.06 us (27%)
    all_to_all x1, starting transfers between devices, body(): lax.all_to_all(blocks, ('var', 'near'), 0, 0, tiled=True)  7.05 us
    pallas_call x1, Pallas kernels, body(): call(functools.partial(block_kernel, pairs), shaped(LATENT, ROWS, COLS, D...  6.73 us
    all_to_all x1, waiting for transfers between devices, body(): lax.all_to_all(blocks, ('var', 'near'), 0, 0, tiled=True)  6.29 us
    ppermute x1, waiting for transfers between devices, body(): beyond = lax.ppermute(mine, ('far', 'near'), swaps)  4.42 us
    pallas_call x1, Pallas kernels, body(): call(own_kernel, (shaped(TOKENS, D), shaped(4, 256, 1024), shaped(TOKENS,...  2.42 us
    pallas_call x1, Pallas kernels, body(): call(fold_kernel, (shaped(128, FOLDED), shaped(LEVELS, D + 128, dtype=F32...  2.25 us
    ppermute x1, starting transfers between devices, body(): beyond = lax.ppermute(mine, ('far', 'near'), swaps)  2.02 us
    pallas_call x1, Pallas kernels, body(): call(blocks_kernel, shaped(2 * LEVELS, 8, WIDE), (pltpu.VMEM(patches.shap...  1.7 us
  transfers between devices with their start and end apart: 2, of which 2 were waited for; matrix products, arithmetic and copies ran while one was open for 0% of the time, Pallas kernels for 14%

profile of v2, /device:TPU:128, one launch (start us, length us, event | category | flops | bytes accessed | tf_op | source)
XLA Modules:
  0.0 33.1 jit_solution(12408492276810975999)
XLA Ops:
  0.0 1.7 %shard_map.136 = bf16[16,8,1024]{2,1,0:T(8,128)(2,1)} custom-call(bf16[1,6,7680]{2,1,0:T(8,128)(2,1)} %pixels.1), custom_call_target="tpu_custom_call" | custom-call | flops 1000000 | bytes 1000000 | tf_op jit(solution)/shard_map/pallas_call | solution.py:224
  1.7 7.0 %all-to-all-start = ((bf16[16,8,1024]{2,1,0:T(8,128)(2,1)}), bf16[16,8,1024]{2,1,0:T(8,128)(2,1)S(1)}, u32[]{:S(2)}, u32[]{:S(2)}) async-start(bf16[16,8,1024]{2,1,0:T(8,128)(2,1)} %shard_map.136), calls=%async_computation | async-start | bytes 524288 | tf_op jit(solution)/shard_map/all_to_all | solution.py:232
  8.8 0.0 copy-start.2
  8.8 0.0 copy-start.3
  8.8 0.0 copy-start.4
  8.8 0.0 copy-start.6
  8.8 0.0 copy-start.7
  8.8 2.3 %shard_map.137 = (bf16[128,768]{1,0:T(8,128)(2,1)S(1)}, f32[8,640]{1,0:T(8,128)S(1)}, bf16[256,1536]{1,0:T(8,128)(2,1)S(1)}) custom-call(bf16[8,512]{1,0:T(8,128)(2,1)} %bias_hbm.1, bf16[80,512]{1,0:T(8,128)(2,1)} %embed_hbm.1, bf16[3,512]{1,0:T(4,128)(2,1)} %query.3, bf16[512,512]{1,0:T(8,128)(2,1)} %key_hbm.1, bf16[512,512]{1,0:T(8,128)(2,1)} %value_hbm.1), custom_call_target="tpu_custom_call" | custom-call | flops 1000000000 | bytes 6000000 | tf_op jit(solution)/shard_map/pallas_call | solution.py:233
  11.1 6.3 %all-to-all-done = bf16[16,8,1024]{2,1,0:T(8,128)(2,1)S(1)} async-done(((bf16[16,8,1024]{2,1,0:T(8,128)(2,1)}), bf16[16,8,1024]{2,1,0:T(8,128)(2,1)S(1)}, u32[]{:S(2)}, u32[]{:S(2)}) %all-to-all-start) | async-done | bytes 262176 | tf_op jit(solution)/shard_map/all_to_all | solution.py:232
  17.4 2.0 %collective-permute-start = (bf16[8,8,1024]{2,1,0:T(8,128)(2,1)S(1)}, bf16[8,8,1024]{2,1,0:T(8,128)(2,1)S(1)}, u32[]{:S(2)}, u32[]{:S(2)}) collective-permute-start(bf16[8,8,1024]{2,1,0:T(8,128)(2,1)S(1)} %dynamic-slice_bitcast_fusion), channel_id=1, source_target_pairs={{2,4},{6,8},{10,12},{14,16},{18,20},{22,24},{26,28},{4,2},{8,6},{1... | collective-permute-start | bytes 393224 | tf_op jit(solution)/shard_map/ppermute | solution.py:254
  19.4 0.0 copy-done.2
  19.4 0.0 copy-done.3
  19.4 0.0 copy-done.4
  19.5 0.0 copy-done.6
  19.5 0.0 copy-done.7
  19.5 0.0 copy-start
  19.5 0.0 copy-start.1
  19.5 0.0 copy-start.5
  19.5 0.0 copy-start.8
  19.5 2.4 %shard_map.138 = (bf16[224,512]{1,0:T(8,128)(2,1)S(1)}, bf16[4,256,1024]{2,1,0:T(8,128)(2,1)S(1)}, bf16[224,1024]{1,0:T(8,128)(2,1)S(1)}) custom-call(bf16[8,2,8,1024]{3,2,1,0:T(8,128)(2,1)S(1)} %bitcast.6, bf16[128,768]{1,0:T(8,128)(2,1)S(1)} %get-tuple-element.11.folded, f32[8,640]{1,0:T(8,128)S(1)} %get-tuple-element.12.folded_bias, ...), custom_call_target="tpu_custom_call" | custom-call | flops 3000000000 | bytes 10000000 | tf_op jit(solution)/shard_map/pallas_call | solution.py:262
  21.9 4.4 %collective-permute-done.beyond = bf16[8,8,1024]{2,1,0:T(8,128)(2,1)S(1)} collective-permute-done((bf16[8,8,1024]{2,1,0:T(8,128)(2,1)S(1)}, bf16[8,8,1024]{2,1,0:T(8,128)(2,1)S(1)}, u32[]{:S(2)}, u32[]{:S(2)}) %collective-permute-start) | collective-permute-done | bytes 131104 | tf_op jit(solution)/shard_map/ppermute | solution.py:254
  26.4 0.0 copy-done
  26.4 0.0 copy-done.1
  26.4 0.0 copy-done.5
  26.4 0.0 copy-done.8
  26.4 6.7 %shard_map.139 = bf16[3,6,12,512]{3,2,1,0:T(8,128)(2,1)} custom-call(bf16[8,2,8,1024]{3,2,1,0:T(8,128)(2,1)S(1)} %bitcast.7, bf16[8,8,1024]{2,1,0:T(8,128)(2,1)S(1)} %collective-permute-done.beyond, bf16[128,768]{1,0:T(8,128)(2,1)S(1)} %get-tuple-element.11.folded, f32[8,640]{1,0:T(8,128)S(1)} %get-tuple-element.12.folded_bias, ...), custom_call_target="tpu_custom_call" | custom-call | flops 4000000000 | bytes 10000000 | tf_op jit(solution)/shard_map/pallas_call | solution.py:269
  (1 shorter events, 0.0 us)
Async XLA Ops:
  1.7 15.7 %all-to-all-start = ((bf16[16,8,1024]{2,1,0:T(8,128)(2,1)}), bf16[16,8,1024]{2,1,0:T(8,128)(2,1)S(1)}, u32[]{:S(2)}, u32[]{:S(2)}) async-start(bf16[16,8,1024]{2,1,0:T(8,128)(2,1)} %shard_map.136), calls=%async_computation | async-start | bytes 524288 | tf_op jit(solution)/shard_map/all_to_all | solution.py:232
  8.8 10.7 %copy-start.2 = (bf16[512,1024]{1,0:T(8,128)(2,1)S(1)}, bf16[512,1024]{1,0:T(8,128)(2,1)}, u32[]{:S(2)}) copy-start(bf16[512,1024]{1,0:T(8,128)(2,1)} %to_context.3) | copy-start | bytes 3145732
  8.8 10.7 %copy-start.3 = (bf16[512,512]{1,0:T(8,128)(2,1)S(1)}, bf16[512,512]{1,0:T(8,128)(2,1)}, u32[]{:S(2)}) copy-start(bf16[512,512]{1,0:T(8,128)(2,1)} %to_query.1) | copy-start | bytes 1572868
  8.8 10.7 %copy-start.4 = (bf16[512,512]{1,0:T(8,128)(2,1)S(1)}, bf16[512,512]{1,0:T(8,128)(2,1)}, u32[]{:S(2)}) copy-start(bf16[512,512]{1,0:T(8,128)(2,1)} %output.3) | copy-start | bytes 1572868
  8.8 10.7 %copy-start.6 = (bf16[3,512]{1,0:T(4,128)(2,1)S(1)}, bf16[3,512]{1,0:T(4,128)(2,1)}, u32[]{:S(2)}) copy-start(bf16[3,512]{1,0:T(4,128)(2,1)} %query.3) | copy-start | bytes 9220
  8.8 10.7 %copy-start.7 = (f32[512]{0:T(512)S(1)}, f32[512]{0:T(512)}, u32[]{:S(2)}) copy-start(f32[512]{0:T(512)} %param.21) | copy-start | bytes 6148
  17.4 9.0 %collective-permute-start = (bf16[8,8,1024]{2,1,0:T(8,128)(2,1)S(1)}, bf16[8,8,1024]{2,1,0:T(8,128)(2,1)S(1)}, u32[]{:S(2)}, u32[]{:S(2)}) collective-permute-start(bf16[8,8,1024]{2,1,0:T(8,128)(2,1)S(1)} %dynamic-slice_bitcast_fusion), channel_id=1, source_target_pairs={{2,4},{6,8},{10,12},{14,16},{18,20},{22,24},{26,28},{4,2},{8,6},{1... | collective-permute-start | bytes 393224 | tf_op jit(solution)/shard_map/ppermute | solution.py:254
  19.5 6.9 %copy-start = (bf16[512,2048]{1,0:T(8,128)(2,1)S(1)}, bf16[512,2048]{1,0:T(8,128)(2,1)}, u32[]{:S(2)}) copy-start(bf16[512,2048]{1,0:T(8,128)(2,1)} %up.1) | copy-start | bytes 6291460
  19.5 6.9 %copy-start.1 = (bf16[2048,512]{1,0:T(8,128)(2,1)S(1)}, bf16[2048,512]{1,0:T(8,128)(2,1)}, u32[]{:S(2)}) copy-start(bf16[2048,512]{1,0:T(8,128)(2,1)} %down.1) | copy-start | bytes 6291460
  19.5 6.9 %copy-start.5 = (bf16[512,512]{1,0:T(8,128)(2,1)S(1)}, bf16[512,512]{1,0:T(8,128)(2,1)}, u32[]{:S(2)}) copy-start(bf16[512,512]{1,0:T(8,128)(2,1)} %mix.1) | copy-start | bytes 1572868
  19.5 6.9 %copy-start.8 = (f32[512]{0:T(512)S(1)}, f32[512]{0:T(512)}, u32[]{:S(2)}) copy-start(f32[512]{0:T(512)} %param.25) | copy-start | bytes 6148

commit v3 on v2

v3 whole, which is shorter than its diff:
```python
import functools
import math

import jax
import jax.numpy as jnp
from jax import lax
from jax.experimental import pallas as pl
from jax.experimental.pallas import tpu as pltpu
from jax.sharding import Mesh
from jax.sharding import PartitionSpec as P

HEADS = 16
HEAD = 32
D = 512
LATENT = 3
LEVELS = 8
ROWS = 6
COLS = 12
PIXELS = 80
WIDE = 1024
HALF = 112
FILLED = 108
TOKENS = 2 * HALF
FOLDED = 768
EPSILON = 1e-05
HALO_TILES = 6
TILES = 9
RATE = HEAD**-0.5 * math.log2(math.e)
F32 = jnp.float32
BF16 = jnp.bfloat16


def dot(a, b):
    return jnp.dot(a, b, preferred_element_type=F32)


def dot_nt(a, b):
    return lax.dot_general(a, b, (((1,), (1,)), ((), ())), preferred_element_type=F32)


def split(a):
    high = a.astype(BF16)
    return high, (a - high.astype(F32)).astype(BF16)


def iota(shape, dim):
    return lax.broadcasted_iota(jnp.int32, shape, dim)


def layer_norm(tensor, scales):
    center = jnp.mean(tensor, axis=-1, keepdims=True)
    offset = tensor - center
    spread = jnp.mean(offset * offset, axis=-1, keepdims=True)
    return offset * lax.rsqrt(spread + EPSILON) * scales


def blocks_kernel(pixels, out, held, arrived):
    copy = pltpu.make_async_copy(pixels, held, arrived)
    copy.start()
    out[...] = jnp.zeros_like(out)
    copy.wait()
    wide = held[0].astype(F32)
    for v in range(LEVELS):
        block = wide[:, v * COLS * PIXELS : (v + 1) * COLS * PIXELS].astype(BF16)
        out[2 * v, :ROWS, : COLS * PIXELS] = block
        out[2 * v + 1, :ROWS, : COLS * PIXELS] = block


def fold_kernel(bias_hbm, embed_hbm, query_hbm, key_hbm, value_hbm, folded, folded_bias, expand,
                bias, embed, query, key, value, arrived):
    pairs = ((query_hbm, query), (key_hbm, key), (embed_hbm, embed), (value_hbm, value), (bias_hbm, bias))
    copies = [pltpu.make_async_copy(*pair, arrived.at[k]) for k, pair in enumerate(pairs)]
    for copy in copies:
        copy.start()
    for q in range(LATENT):
        lane = (iota((256, D), 1) >> 5) + q * HEADS
        expand[:, q * D : (q + 1) * D] = jnp.where((iota((256, D), 0) & 127) == lane, 1.0, 0.0).astype(BF16)
    for copy in copies:
        copy.wait()
    own = iota((HEADS, D), 1) // HEAD == iota((HEADS, D), 0)
    spread = [jnp.where(own, query[q : q + 1].astype(F32), 0.0) for q in range(LATENT)]
    spread.append(jnp.zeros((128 - LATENT * HEADS, D), F32))
    spread = jnp.concatenate(spread, axis=0).astype(BF16)
    high, low = split(dot_nt(key[...], spread))
    scores = dot(embed[...], high) + dot(embed[...], low)
    high_score, low_score = split(scores)
    folded[PIXELS:] = jnp.zeros((128 - PIXELS, FOLDED), BF16)
    folded[:PIXELS, :D] = dot(embed[...], value[...]).astype(BF16)
    folded[:PIXELS, D : D + 128] = high_score
    folded[:PIXELS, D + 128 :] = low_score
    folded_bias[:, :D] = dot(bias[...], value[...])
    folded_bias[:, D:] = dot(bias[...], high) + dot(bias[...], low)


def pick_own(near):
    source = iota((1, LATENT * TILES * 8), 1)
    q = (source >= TILES * 8).astype(jnp.int32) + (source >= 2 * TILES * 8).astype(jnp.int32)
    source = source - TILES * 8 * q
    tile, place = source >> 3, source & 7
    group = (tile >= 3).astype(jnp.int32) + (tile >= 6).astype(jnp.int32)
    member = tile - 3 * group
    j = 4 * group + jnp.where(place < ROWS, member, 3)
    row = jnp.where(place < ROWS, place, 2 * member + place - ROWS)
    lower = (row >= 3).astype(jnp.int32)
    half = jnp.where(lower == near, 1, 0)
    source = half * HALF + (q * 3 + row - 3 * lower) * COLS + j
    target = iota((TOKENS, 1), 0)
    spare = jnp.where(target >= HALF, target - HALF, target) >= FILLED
    target = jnp.where(spare, target - (HALF - FILLED), target)
    return jnp.where(source == target, 1.0, 0.0).astype(BF16)


def pick_halo():
    source = iota((1, LATENT * HALO_TILES * 8), 1)
    q = (source >= HALO_TILES * 8).astype(jnp.int32) + (source >= 2 * HALO_TILES * 8).astype(jnp.int32)
    source = source - HALO_TILES * 8 * q
    tile, place = source >> 3, source & 7
    second = (place >= 3).astype(jnp.int32)
    source = jnp.where(place < 6, (q * 3 + place - 3 * second) * COLS + 2 * tile + second, -1)
    target = iota((HALF, 1), 0)
    target = jnp.where(target >= FILLED, target - (HALF - FILLED), target)
    return jnp.where(source == target, 1.0, 0.0).astype(BF16)


def patches_of(x, first, last):
    return [x[:, :, j * PIXELS : j * PIXELS + 128] for j in range(first, last)]


def own_rows(x, rows):
    full = iota((LEVELS, 8, 128), 1) < ROWS
    for group in range(3):
        four = patches_of(x, 4 * group, 4 * group + 4)
        for member in range(3):
            tile = jnp.where(full, four[member], pltpu.roll(four[3], ROWS - 2 * member, 1))
            start = (group * 3 + member) * 64
            rows[start : start + 64] = tile.reshape(64, 128).astype(BF16)


def halo_rows(x, lower, rows):
    x = jnp.where(lower, pltpu.roll(x, 5, 1), x)
    first = iota((LEVELS, 8, 128), 1) < 3
    for pair in range(HALO_TILES):
        left, right = patches_of(x, 2 * pair, 2 * pair + 2)
        tile = jnp.where(first, left, pltpu.roll(right, 3, 1))
        rows[pair * 64 : (pair + 1) * 64] = tile.reshape(64, 128).astype(BF16)


def pool(folded, folded_bias, expand, rows, values, weights, pooled):
    tiles = rows.shape[0] // 64
    both = dot(rows[...], folded[:, D:])
    score = (both[:, :128] + both[:, 128:]).reshape(tiles, LEVELS, 8, 128) + folded_bias[:, D:][None, :, None, :]
    share = jnp.exp2((score - jnp.max(score, axis=1, keepdims=True)) * RATE)
    share = share / jnp.sum(share, axis=1, keepdims=True)
    high, low = split(share.reshape(tiles * 64, 128))
    weights[:, :128] = high
    weights[:, 128:] = low
    values[...] = dot(rows[...], folded[:, :D]).reshape(tiles, LEVELS, 8, D) + folded_bias[:, :D][None, :, None, :]
    for q in range(LATENT):
        full = dot(weights[...], expand[:, q * D : (q + 1) * D]).reshape(tiles, LEVELS, 8, D)
        total = jnp.sum(full * values[...], axis=1).astype(BF16)
        start = 0
        for array in pooled:
            size = array.shape[0] // LATENT
            array[q * size : (q + 1) * size] = total[start : start + size // 8].reshape(size, D)
            start += size // 8


def latent_rows(picked, query, output):
    place = iota((HALF, 1), 0)
    first, second, third = (query[q : q + 1].astype(F32) for q in range(LATENT))
    added = jnp.where(place < 36, first, jnp.where(place < 72, second, third))
    added = jnp.concatenate([added] * (picked.shape[0] // HALF), axis=0)
    return (dot(picked.astype(BF16), output[...]) + added).astype(BF16)


def spread_heads(queries, spread):
    part = jnp.concatenate([queries, jnp.zeros((128 - HALF, D), F32)], axis=0).T.astype(BF16)
    spread[...] = jnp.zeros_like(spread)
    for head in range(HEADS):
        group, spot = divmod(head, 4)
        spread[group, spot * HEAD : (spot + 1) * HEAD, spot * 128 : (spot + 1) * 128] = (
            part[head * HEAD : (head + 1) * HEAD]
        )


def attend(spread, own, beside, there):
    lane = iota((1, TOKENS), 1)
    filled = jnp.where(lane >= HALF, lane - HALF, lane) < FILLED
    usable = jnp.where(filled & ((lane < HALF) | there), 1.0, 0.0)
    keys = jnp.concatenate([own[:, :D], jnp.where(there, beside[:, :D], own[:, :D])], axis=0)
    turned = jnp.concatenate([own[:, D:], beside[:, D:]], axis=0).astype(F32).T
    turned = jnp.where(usable > 0.0, turned, 0.0).astype(BF16)
    count = jnp.broadcast_to(usable, (16, TOKENS)).astype(BF16)
    parts = []
    for group in range(4):
        score = dot(keys[:, group * 128 : (group + 1) * 128], spread[group])
        share = jnp.exp2((score - jnp.max(score, axis=0, keepdims=True)) * RATE).astype(BF16)
        for pair in range(2):
            start = (group * 2 + pair) * 2 * HEAD
            weighed = jnp.concatenate([turned[start : start + 2 * HEAD], count], axis=0)
            got = dot(weighed, share[:, pair * 256 : (pair + 1) * 256])
            inverse = 1.0 / got[2 * HEAD : 2 * HEAD + 1]
            parts.append(got[:HEAD, :128] * inverse[:, :128])
            parts.append(got[HEAD : 2 * HEAD, 128:] * inverse[:, 128:])
    return jnp.concatenate(parts, axis=0).T[:HALF].astype(BF16)


def own_kernel(x, folded, folded_bias, expand, query, output, gain, to_query, to_context,
               latent, attended, spread_query, context, rows, values, weights, pooled, halo_pooled, spread_here):
    near = lax.axis_index("near")
    own_rows(x[:, pl.ds(near, 1)].reshape(LEVELS, 8, WIDE).astype(F32), rows.at[: TILES * 64])
    halo_rows(x[:, pl.ds(1 - near, 1)].reshape(LEVELS, 8, WIDE).astype(F32), near == 1, rows.at[TILES * 64 :])
    pool(folded, folded_bias, expand, rows, values, weights, (pooled, halo_pooled))
    picked = jnp.concatenate([dot(pick_own(near), pooled[...]), dot(pick_halo(), halo_pooled[...])], axis=0)
    tokens = latent_rows(picked, query, output)
    latent[...] = tokens[:TOKENS]
    normed = layer_norm(tokens.astype(F32), gain[...]).astype(BF16)
    queries = dot(normed[:TOKENS], to_query[...]).astype(BF16).astype(F32)
    seen = dot(normed, to_context[...]).astype(BF16)
    context[...] = seen[HALF:TOKENS]
    spread_heads(queries[HALF:], spread_query)
    spread_heads(queries[:HALF], spread_here)
    attended[...] = attend(spread_here, seen[:HALF], seen[TOKENS:], True)


def block_kernel(pairs, beyond, folded, folded_bias, expand, query, output, gain, to_context, latent, attended,
                 spread_query, context, mix, second_gain, up, down, out, rows, values, weights, halo_pooled):
    near = lax.axis_index("near")
    band = lax.axis_index("far") * 2 + near
    halo_rows(beyond[...].astype(F32), near == 0, rows)
    pool(folded, folded_bias, expand, rows, values, weights, (halo_pooled,))
    tokens = latent_rows(dot(pick_halo(), halo_pooled[...]), query, output)
    normed = layer_norm(tokens.astype(F32), gain[...]).astype(BF16)
    beside = dot(normed, to_context[...]).astype(BF16)
    there = (band > 0) & (band < 2 * pairs - 1)
    second_half = attend(spread_query, context[...], beside, there)
    both = jnp.concatenate([attended[...], second_half], axis=0)
    mixed = dot(both, mix[...]) + latent[...].astype(F32)
    second = layer_norm(mixed, second_gain[...]).astype(BF16)
    hidden = jax.nn.gelu(dot(second, up[...])).astype(BF16)
    result = mixed + dot(hidden, down[...])
    for half in range(2):
        first_row = (1 - near if half == 0 else near) * 3
        for q in range(LATENT):
            for i in range(3):
                start = half * HALF + (q * 3 + i) * COLS
                out[q, pl.ds(first_row + i, 1)] = result[start : start + COLS].astype(BF16)[None]


def call(kernel, outs, scratch=(), flops=0, moved=0, limit=24, hbm=0):
    specs = {"in_specs": [pl.BlockSpec(memory_space=pltpu.HBM)] * hbm} if hbm else {}
    return pl.pallas_call(
        kernel,
        out_shape=outs,
        scratch_shapes=list(scratch),
        compiler_params=pltpu.CompilerParams(vmem_limit_bytes=limit * 2**20),
        cost_estimate=pl.CostEstimate(flops=flops, bytes_accessed=moved, transcendentals=0),
        **specs,
    )


def shaped(*shape, dtype=BF16):
    return jax.ShapeDtypeStruct(shape, dtype)


def body(
    patches,
    level_bias,
    embed_weight,
    latent_query,
    cross_key,
    cross_value,
    cross_output,
    first_gain,
    window_query,
    window_context,
    window_output,
    second_gain,
    up_weight,
    down_weight,
):
    pairs = lax.axis_size("far")
    blocks = call(
        blocks_kernel,
        shaped(2 * LEVELS, 8, WIDE),
        (pltpu.VMEM(patches.shape, BF16), pltpu.SemaphoreType.DMA),
        flops=10**6,
        moved=10**6,
        hbm=1,
    )(pltpu.with_memory_space_constraint(patches, pltpu.HBM))
    x = lax.all_to_all(blocks, ("var", "near"), 0, 0, tiled=True).reshape(LEVELS, 2, 8, WIDE)
    folded, folded_bias, expand = call(
        fold_kernel,
        (
            shaped(128, FOLDED),
            shaped(LEVELS, D + 128, dtype=F32),
            shaped(256, LATENT * D),
        ),
        tuple(pltpu.VMEM(a.shape, BF16) for a in (level_bias, embed_weight, latent_query, cross_key, cross_value))
        + (pltpu.SemaphoreType.DMA((5,)),),
        flops=10**9,
        moved=6 * 10**6,
        hbm=5,
    )(
        *(
            pltpu.with_memory_space_constraint(a, pltpu.HBM)
            for a in (level_bias, embed_weight, latent_query, cross_key, cross_value)
        )
    )
    swaps = [(2 * k + 1, 2 * k + 2) for k in range(pairs - 1)]
    swaps += [(b, a) for a, b in swaps]
    mine = lax.dynamic_index_in_dim(x, lax.axis_index("near"), 1, keepdims=False)
    beyond = lax.ppermute(mine, ("far", "near"), swaps)
    def pool_scratch(tiles):
        return (
            pltpu.VMEM((tiles * 64, 128), BF16),
            pltpu.VMEM((tiles, LEVELS, 8, D), F32),
            pltpu.VMEM((tiles * 64, 256), BF16),
        )

    halo_pooled = pltpu.VMEM((LATENT * HALO_TILES * 8, D), BF16)
    gain = first_gain.reshape(1, D)
    latent, attended, spread_query, context = call(
        own_kernel,
        (shaped(TOKENS, D), shaped(HALF, D), shaped(4, 128, 512), shaped(HALF, 2 * D)),
        (*pool_scratch(TILES + HALO_TILES), pltpu.VMEM((LATENT * TILES * 8, D), BF16), halo_pooled,
         pltpu.VMEM((4, 128, 512), BF16)),
        flops=3 * 10**9,
        moved=10**7,
    )(x, folded, folded_bias, expand, latent_query, cross_output, gain, window_query, window_context)
    return call(
        functools.partial(block_kernel, pairs),
        shaped(LATENT, ROWS, COLS, D),
        (*pool_scratch(HALO_TILES), halo_pooled),
        flops=4 * 10**9,
        moved=10**7,
    )(beyond, folded, folded_bias, expand, latent_query, cross_output, gain, window_context, latent, attended,
      spread_query, context, window_output, second_gain.reshape(1, D), up_weight, down_weight)


def solution(mesh):
    finer = Mesh(
        mesh.devices.reshape(mesh.shape["var"], mesh.shape["lat"] // 2, 2, mesh.shape["dp"]),
        ("var", "far", "near", "dp"),
    )
    return jax.shard_map(
        body,
        mesh=finer,
        in_specs=(P(("dp", "var"), ("far", "near"), None),) + (P(),) * 13,
        out_specs=P("dp", ("far", "near"), "var", None),
        check_vma=False,
    )
```

time: 33.4 us -> 32.2 us (0.964)
  the two profiles are of different devices: /device:TPU:128 before, /device:TPU:104 now
where the time goes in v3:
time: 32.2 us; the launch traced here: 32 us
  Pallas kernels  13.4 us (42%)
  starting transfers between devices  13.3 us (41%)
  waiting for transfers between devices  4.94 us (15%)
    all_to_all x1, starting transfers between devices, body(): lax.all_to_all(blocks, ('var', 'near'), 0, 0, tiled=True)  7.4 us
    ppermute x1, starting transfers between devices, body(): beyond = lax.ppermute(mine, ('far', 'near'), swaps)  5.93 us
    pallas_call x1, Pallas kernels, body(): call(functools.partial(block_kernel, pairs), shaped(LATENT, ROWS, COLS, D...  5.21 us
    all_to_all x1, waiting for transfers between devices, body(): lax.all_to_all(blocks, ('var', 'near'), 0, 0, tiled=True)  4.94 us
    pallas_call x1, Pallas kernels, body(): call(own_kernel, (shaped(TOKENS, D), shaped(HALF, D), shaped(4, 128, 512)...  4.27 us
    pallas_call x1, Pallas kernels, body(): call(fold_kernel, (shaped(128, FOLDED), shaped(LEVELS, D + 128, dtype=F32...  2.26 us
    pallas_call x1, Pallas kernels, body(): call(blocks_kernel, shaped(2 * LEVELS, 8, WIDE), (pltpu.VMEM(patches.shap...  1.7 us
  transfers between devices with their start and end apart: 2, of which 1 were waited for; matrix products, arithmetic and copies ran while one was open for 0% of the time, Pallas kernels for 20%

profile of v3, /device:TPU:104, one launch (start us, length us, event | category | flops | bytes accessed | tf_op | source)
XLA Modules:
  0.0 32.0 jit_solution(4007205031629672264)
XLA Ops:
  0.0 1.7 %shard_map.136 = bf16[16,8,1024]{2,1,0:T(8,128)(2,1)} custom-call(bf16[1,6,7680]{2,1,0:T(8,128)(2,1)} %pixels.1), custom_call_target="tpu_custom_call" | custom-call | flops 1000000 | bytes 1000000 | tf_op jit(solution)/shard_map/pallas_call | solution.py:283
  1.7 7.4 %all-to-all-start = ((bf16[16,8,1024]{2,1,0:T(8,128)(2,1)}), bf16[16,8,1024]{2,1,0:T(8,128)(2,1)S(1)}, u32[]{:S(2)}, u32[]{:S(2)}) async-start(bf16[16,8,1024]{2,1,0:T(8,128)(2,1)} %shard_map.136), calls=%async_computation | async-start | bytes 524288 | tf_op jit(solution)/shard_map/all_to_all | solution.py:291
  9.1 0.0 copy-start.2
  9.1 0.0 copy-start.3
  9.1 0.0 copy-start.4
  9.1 0.0 copy-start.6
  9.2 0.0 copy-start.7
  9.2 2.3 %shard_map.137 = (bf16[128,768]{1,0:T(8,128)(2,1)S(1)}, f32[8,640]{1,0:T(8,128)S(1)}, bf16[256,1536]{1,0:T(8,128)(2,1)S(1)}) custom-call(bf16[8,512]{1,0:T(8,128)(2,1)} %bias_hbm.1, bf16[80,512]{1,0:T(8,128)(2,1)} %embed_hbm.1, bf16[3,512]{1,0:T(4,128)(2,1)} %query.3, bf16[512,512]{1,0:T(8,128)(2,1)} %key_hbm.1, bf16[512,512]{1,0:T(8,128)(2,1)} %value_hbm.1), custom_call_target="tpu_custom_call" | custom-call | flops 1000000000 | bytes 6000000 | tf_op jit(solution)/shard_map/pallas_call | solution.py:292
  11.4 4.9 %all-to-all-done = bf16[16,8,1024]{2,1,0:T(8,128)(2,1)S(1)} async-done(((bf16[16,8,1024]{2,1,0:T(8,128)(2,1)}), bf16[16,8,1024]{2,1,0:T(8,128)(2,1)S(1)}, u32[]{:S(2)}, u32[]{:S(2)}) %all-to-all-start) | async-done | bytes 262176 | tf_op jit(solution)/shard_map/all_to_all | solution.py:291
  16.4 5.9 %collective-permute-start = (bf16[8,8,1024]{2,1,0:T(8,128)(2,1)S(1)}, bf16[8,8,1024]{2,1,0:T(8,128)(2,1)S(1)}, u32[]{:S(2)}, u32[]{:S(2)}) collective-permute-start(bf16[8,8,1024]{2,1,0:T(8,128)(2,1)S(1)} %dynamic-slice_bitcast_fusion), channel_id=1, source_target_pairs={{2,4},{6,8},{10,12},{14,16},{18,20},{22,24},{26,28},{4,2},{8,6},{1... | collective-permute-start | bytes 393224 | tf_op jit(solution)/shard_map/ppermute | solution.py:313
  22.3 0.0 copy-done.2
  22.3 0.0 copy-done.3
  22.3 0.0 copy-done.4
  22.4 0.0 copy-done.6
  22.4 0.0 copy-done.7
  22.4 0.0 copy-start
  22.4 0.0 copy-start.1
  22.4 0.0 copy-start.5
  22.4 0.0 copy-start.8
  22.4 4.3 %shard_map.138 = (bf16[224,512]{1,0:T(8,128)(2,1)S(1)}, bf16[112,512]{1,0:T(8,128)(2,1)S(1)}, bf16[4,128,512]{2,1,0:T(8,128)(2,1)S(1)}, bf16[112,1024]{1,0:T(8,128)(2,1)S(1)}) custom-call(bf16[8,2,8,1024]{3,2,1,0:T(8,128)(2,1)S(1)} %bitcast.6, bf16[128,768]{1,0:T(8,128)(2,1)S(1)} %get-tuple-element.12.folded, f32[8,640]{1,0:T(8,128)S(1)} %get-tuple-element.13.folded_bias, ...), custom_call_target="tpu_custom_call" | custom-call | flops 3000000000 | bytes 10000000 | tf_op jit(solution)/shard_map/pallas_call | solution.py:323
  26.7 0.0 collective-permute-done.beyond
  26.7 0.0 copy-done
  26.7 0.0 copy-done.1
  26.7 0.0 copy-done.5
  26.7 0.0 copy-done.8
  26.7 5.2 %shard_map.139 = bf16[3,6,12,512]{3,2,1,0:T(8,128)(2,1)} custom-call(bf16[8,8,1024]{2,1,0:T(8,128)(2,1)S(1)} %collective-permute-done.beyond, bf16[128,768]{1,0:T(8,128)(2,1)S(1)} %get-tuple-element.12.folded, f32[8,640]{1,0:T(8,128)S(1)} %get-tuple-element.13.folded_bias, bf16[256,1536]{1,0:T(8,128)(2,1)S(1)} %get-tuple-element.14.expand, ...), custom_call_target="tpu_custom_call" | custom-call | flops 4000000000 | bytes 10000000 | tf_op jit(solution)/shard_map/pallas_call | solution.py:331
  (1 shorter events, 0.0 us)
Async XLA Ops:
  1.7 14.7 %all-to-all-start = ((bf16[16,8,1024]{2,1,0:T(8,128)(2,1)}), bf16[16,8,1024]{2,1,0:T(8,128)(2,1)S(1)}, u32[]{:S(2)}, u32[]{:S(2)}) async-start(bf16[16,8,1024]{2,1,0:T(8,128)(2,1)} %shard_map.136), calls=%async_computation | async-start | bytes 524288 | tf_op jit(solution)/shard_map/all_to_all | solution.py:291
  9.1 13.2 %copy-start.2 = (bf16[512,1024]{1,0:T(8,128)(2,1)S(1)}, bf16[512,1024]{1,0:T(8,128)(2,1)}, u32[]{:S(2)}) copy-start(bf16[512,1024]{1,0:T(8,128)(2,1)} %to_context.3) | copy-start | bytes 3145732
  9.1 13.2 %copy-start.3 = (bf16[512,512]{1,0:T(8,128)(2,1)S(1)}, bf16[512,512]{1,0:T(8,128)(2,1)}, u32[]{:S(2)}) copy-start(bf16[512,512]{1,0:T(8,128)(2,1)} %to_query.1) | copy-start | bytes 1572868
  9.1 13.2 %copy-start.4 = (bf16[512,512]{1,0:T(8,128)(2,1)S(1)}, bf16[512,512]{1,0:T(8,128)(2,1)}, u32[]{:S(2)}) copy-start(bf16[512,512]{1,0:T(8,128)(2,1)} %output.3) | copy-start | bytes 1572868
  9.1 13.2 %copy-start.6 = (bf16[3,512]{1,0:T(4,128)(2,1)S(1)}, bf16[3,512]{1,0:T(4,128)(2,1)}, u32[]{:S(2)}) copy-start(bf16[3,512]{1,0:T(4,128)(2,1)} %query.3) | copy-start | bytes 9220
  9.2 13.2 %copy-start.7 = (f32[512]{0:T(512)S(1)}, f32[512]{0:T(512)}, u32[]{:S(2)}) copy-start(f32[512]{0:T(512)} %param.21) | copy-start | bytes 6148
  16.4 10.3 %collective-permute-start = (bf16[8,8,1024]{2,1,0:T(8,128)(2,1)S(1)}, bf16[8,8,1024]{2,1,0:T(8,128)(2,1)S(1)}, u32[]{:S(2)}, u32[]{:S(2)}) collective-permute-start(bf16[8,8,1024]{2,1,0:T(8,128)(2,1)S(1)} %dynamic-slice_bitcast_fusion), channel_id=1, source_target_pairs={{2,4},{6,8},{10,12},{14,16},{18,20},{22,24},{26,28},{4,2},{8,6},{1... | collective-permute-start | bytes 393224 | tf_op jit(solution)/shard_map/ppermute | solution.py:313
  22.4 4.3 %copy-start = (bf16[512,2048]{1,0:T(8,128)(2,1)S(1)}, bf16[512,2048]{1,0:T(8,128)(2,1)}, u32[]{:S(2)}) copy-start(bf16[512,2048]{1,0:T(8,128)(2,1)} %up.1) | copy-start | bytes 6291460
  22.4 4.3 %copy-start.1 = (bf16[2048,512]{1,0:T(8,128)(2,1)S(1)}, bf16[2048,512]{1,0:T(8,128)(2,1)}, u32[]{:S(2)}) copy-start(bf16[2048,512]{1,0:T(8,128)(2,1)} %down.1) | copy-start | bytes 6291460
  22.4 4.3 %copy-start.5 = (bf16[512,512]{1,0:T(8,128)(2,1)S(1)}, bf16[512,512]{1,0:T(8,128)(2,1)}, u32[]{:S(2)}) copy-start(bf16[512,512]{1,0:T(8,128)(2,1)} %mix.1) | copy-start | bytes 1572868
  22.4 4.3 %copy-start.8 = (f32[512]{0:T(512)S(1)}, f32[512]{0:T(512)}, u32[]{:S(2)}) copy-start(f32[512]{0:T(512)} %param.25) | copy-start | bytes 6148

commit v4 on v3

v4 whole, which is shorter than its diff:
```python
import functools
import math

import jax
import jax.numpy as jnp
from jax import lax
from jax.experimental import pallas as pl
from jax.experimental.pallas import tpu as pltpu
from jax.sharding import Mesh
from jax.sharding import PartitionSpec as P

HEADS = 16
HEAD = 32
D = 512
LATENT = 3
LEVELS = 8
ROWS = 6
COLS = 12
PIXELS = 80
PART = 12
PLACES = 40
HALF = 112
FILLED = 108
TOKENS = 2 * HALF
FOLDED = 608
SCORES = 48
EPSILON = 1e-05
MASKED = -1e30
RATE = HEAD**-0.5 * math.log2(math.e)
F32 = jnp.float32
BF16 = jnp.bfloat16


def dot(a, b):
    return jnp.dot(a, b, preferred_element_type=F32)


def dot_nt(a, b):
    return lax.dot_general(a, b, (((1,), (1,)), ((), ())), preferred_element_type=F32)


def split(a):
    high = a.astype(BF16)
    return high, (a - high.astype(F32)).astype(BF16)


def iota(shape, dim):
    return lax.broadcasted_iota(jnp.int32, shape, dim)


def layer_norm(tensor, scales):
    center = jnp.mean(tensor, axis=-1, keepdims=True)
    offset = tensor - center
    spread = jnp.mean(offset * offset, axis=-1, keepdims=True)
    return offset * lax.rsqrt(spread + EPSILON) * scales


def blocks_kernel(pixels, out, held, wide, rows, staged, arrived, left):
    copy = pltpu.make_async_copy(pixels.at[0], held, arrived)
    copy.start()
    length = held.shape[1]
    wide[:, length:] = jnp.zeros((ROWS, 128), F32)
    copy.wait()
    wide[:, :length] = held[...].astype(F32)
    copies = []
    for v in range(LEVELS):
        for group in range(COLS // 3):
            start = (v * COLS + 3 * group) * PIXELS
            patches = wide[:, start : start + 256]
            rows[v, 3 * group : 3 * group + 3] = patches[:3]
            rows[v, PART + 3 * group : PART + 3 * group + 3] = patches[3:]
        staged[v] = rows[v].astype(BF16)
        for k in range(2):
            copies.append(pltpu.make_async_copy(staged.at[v], out.at[2 * v + k], left.at[2 * v + k]))
            copies[-1].start()
    for copy in copies:
        copy.wait()


def fold_kernel(bias_hbm, embed_hbm, query_hbm, key_hbm, value_hbm, folded, bias, embed, query, key, value, arrived):
    pairs = ((query_hbm, query), (key_hbm, key), (embed_hbm, embed), (value_hbm, value), (bias_hbm, bias))
    copies = [pltpu.make_async_copy(*pair, arrived.at[k]) for k, pair in enumerate(pairs)]
    for copy in copies:
        copy.start()
    for copy in copies:
        copy.wait()
    own = iota((HEADS, D), 1) // HEAD == iota((HEADS, D), 0)
    spread = [jnp.where(own, query[q : q + 1].astype(F32), 0.0) for q in range(LATENT)]
    spread = jnp.concatenate(spread * 2 + [jnp.zeros((128 - 2 * SCORES, D), F32)], axis=0).astype(BF16)
    high, low = split(dot_nt(key[...], spread))
    scores = dot(embed[...], high) + dot(embed[...], low)
    bias_scores = dot(bias[...], high) + dot(bias[...], low)
    high_score, low_score = split(scores)
    lane = iota((1, 128), 1)
    first = jnp.where(lane < SCORES, high_score.astype(F32), low_score.astype(F32))
    bias_high, bias_low = (jnp.where(lane < SCORES, part.astype(F32), 0.0) for part in split(bias_scores))
    value_high, value_low = (part.astype(F32) for part in split(dot(bias[...], value[...])))
    rest = jnp.zeros((128 - PIXELS - 2 * LEVELS, D + 128), F32)
    whole = jnp.concatenate(
        [
            jnp.concatenate([dot(embed[...], value[...]), first], axis=1),
            jnp.concatenate([value_high, bias_high], axis=1),
            jnp.concatenate([value_low, bias_low], axis=1),
            rest,
        ],
        axis=0,
    )
    folded[...] = whole.T[:FOLDED].astype(BF16)


def thirds(lane):
    part = (lane >= PLACES).astype(jnp.int32) + (lane >= 2 * PLACES).astype(jnp.int32)
    return part, lane - PLACES * part


def token_of(place, column):
    group = (place * 171) >> 9
    return (place - 3 * group) * COLS + 3 * group + column


def pick_first(near):
    source = iota((1, LATENT * 128), 1)
    q = source >> 7
    column, place = thirds(source & 127)
    part = (place >= PART).astype(jnp.int32) + (place >= 2 * PART).astype(jnp.int32)
    half = jnp.where(part == 2, 2, jnp.where(part == near, 1, 0))
    token = half * HALF + q * 36 + token_of(place - PART * part, column)
    source = jnp.where((place < 3 * PART) & (column < 3), token, -1)
    source = jnp.where((iota((1, LATENT * 128), 1) & 127) < 3 * PLACES, source, -1)
    target = iota((3 * HALF, 1), 0)
    within = target - HALF * ((target >= HALF).astype(jnp.int32) + (target >= 2 * HALF).astype(jnp.int32))
    target = jnp.where(within >= FILLED, target - (HALF - FILLED), target)
    return jnp.where(source == target, 1.0, 0.0).astype(BF16)


def pick_halo():
    source = iota((1, LATENT * 128), 1)
    q = source >> 7
    _, place = thirds(source & 127)
    column = (place >= PART).astype(jnp.int32) + (place >= 2 * PART).astype(jnp.int32)
    token = q * 36 + token_of(place - PART * column, column)
    source = jnp.where(place < 3 * PART, token, -1)
    source = jnp.where((iota((1, LATENT * 128), 1) & 127) < 3 * PLACES, source, -1)
    target = iota((HALF, 1), 0)
    target = jnp.where(target >= FILLED, target - (HALF - FILLED), target)
    return jnp.where(source == target, 1.0, 0.0).astype(BF16)


def single_patches(x, level):
    lane = iota((1, 128), 1)
    marks = jnp.where((lane == PIXELS + level) | (lane == PIXELS + LEVELS + level), 1.0, 0.0)
    patches = (x[:, :128], x[:, PIXELS : PIXELS + 128], pltpu.roll(x[:, 128:], 256 - 2 * PIXELS, 1))
    return [jnp.where(lane < PIXELS, patch, marks) for patch in patches]


def level_scores(values, step):
    lanes = slice(step * 128, (step + 1) * 128)
    return values[D : D + SCORES, lanes] + values[D + SCORES :, lanes]


def weigh(values, weights, pooled):
    for head in range(HEADS):
        rows = slice(head * HEAD, (head + 1) * HEAD)
        totals = [None] * LATENT
        for step in range(weights.shape[0]):
            value = values[rows, step * 128 : (step + 1) * 128]
            for q in range(LATENT):
                place = q * HEADS + head
                term = value * weights[step, place : place + 1]
                totals[q] = term if step == 0 else totals[q] + term
        for q in range(LATENT):
            pooled[rows, q * 128 : (q + 1) * 128] = totals[q].astype(BF16)


def pool_levels(x, folded, values, weights, pooled):
    values[...] = dot_nt(folded[...], x)
    scores = [level_scores(values, step) for step in range(LEVELS)]
    highest = functools.reduce(jnp.maximum, scores)
    shares = [jnp.exp2((score - highest) * RATE) for score in scores]
    inverse = 1.0 / sum(shares)
    for step in range(LEVELS):
        weights[step] = shares[step] * inverse
    weigh(values, weights, pooled)


def over_parts(a, function):
    lane = iota(a.shape, 1)
    after = jnp.where(lane < 2 * PLACES, pltpu.roll(a, 128 - PLACES, 1), pltpu.roll(a, 2 * PLACES, 1))
    before = jnp.where(lane < PLACES, pltpu.roll(a, 128 - 2 * PLACES, 1), pltpu.roll(a, PLACES, 1))
    return function(function(a, after), before)


def pool_parts(x, folded, values, weights, pooled):
    values[...] = dot_nt(folded[...], x)
    scores = [level_scores(values, step) for step in range(3)]
    scores[2] = jnp.where(iota(scores[2].shape, 1) < 2 * PLACES, scores[2], MASKED)
    highest = over_parts(functools.reduce(jnp.maximum, scores), jnp.maximum)
    shares = [jnp.exp2((score - highest) * RATE) for score in scores]
    inverse = 1.0 / over_parts(sum(shares), jnp.add)
    for step in range(3):
        weights[step] = shares[step] * inverse
    weigh(values, weights, pooled)


def latent_rows(picked, query, output):
    place = iota((HALF, 1), 0)
    first, second, third = (query[q : q + 1].astype(F32) for q in range(LATENT))
    added = jnp.where(place < 36, first, jnp.where(place < 72, second, third))
    added = jnp.concatenate([added] * (picked.shape[0] // HALF), axis=0)
    return (dot(picked.astype(BF16), output[...]) + added).astype(BF16)


def spread_heads(queries, spread):
    part = jnp.concatenate([queries, jnp.zeros((128 - HALF, D), F32)], axis=0).T.astype(BF16)
    spread[...] = jnp.zeros_like(spread)
    for head in range(HEADS):
        group, spot = divmod(head, 4)
        spread[group, spot * HEAD : (spot + 1) * HEAD, spot * 128 : (spot + 1) * 128] = (
            part[head * HEAD : (head + 1) * HEAD]
        )


def attend(spread, own, beside, there):
    lane = iota((1, TOKENS), 1)
    filled = jnp.where(lane >= HALF, lane - HALF, lane) < FILLED
    usable = jnp.where(filled & ((lane < HALF) | there), 1.0, 0.0)
    keys = jnp.concatenate([own[:, :D], jnp.where(there, beside[:, :D], own[:, :D])], axis=0)
    turned = jnp.concatenate([own[:, D:], beside[:, D:]], axis=0).astype(F32).T
    turned = jnp.where(usable > 0.0, turned, 0.0).astype(BF16)
    count = jnp.broadcast_to(usable, (16, TOKENS)).astype(BF16)
    scores = [dot(keys[:, group * 128 : (group + 1) * 128], spread[group]) for group in range(4)]
    shares = [jnp.exp2((score - jnp.max(score, axis=0, keepdims=True)) * RATE).astype(BF16) for score in scores]
    parts = []
    for pair in range(HEADS // 2):
        weighed = jnp.concatenate([turned[pair * 2 * HEAD : (pair + 1) * 2 * HEAD], count], axis=0)
        got = dot(weighed, shares[pair // 2][:, pair % 2 * 256 : (pair % 2 + 1) * 256])
        inverse = 1.0 / got[2 * HEAD : 2 * HEAD + 1]
        parts.append(got[:HEAD, :128] * inverse[:, :128])
        parts.append(got[HEAD : 2 * HEAD, 128:] * inverse[:, 128:])
    return jnp.concatenate(parts, axis=0).T[:HALF].astype(BF16)


def own_kernel(x, folded, query, output, gain, to_query, to_context, latent, attended, spread_query, context,
               rows, values, weights, pooled, spread_here):
    near = lax.axis_index("near")
    for level in range(LEVELS):
        own = x[level, pl.ds(near, 1)].reshape(2 * PART, 256).astype(F32)
        other = x[level, pl.ds(1 - near, 1)].reshape(2 * PART, 256).astype(F32)
        halo = jnp.where(near == 1, other[PART:], other[:PART])
        patches = single_patches(jnp.concatenate([own, halo, jnp.zeros((4, 256), F32)], axis=0), level)
        rows[level] = jnp.concatenate([*patches, jnp.zeros((8, 128), F32)], axis=0).astype(BF16)
    pool_levels(rows[...].reshape(LEVELS * 128, 128), folded, values, weights, pooled)
    picked = dot_nt(pick_first(near), pooled[...])
    tokens = latent_rows(picked, query, output)
    latent[...] = tokens[:TOKENS]
    normed = layer_norm(tokens.astype(F32), gain[...]).astype(BF16)
    queries = dot(normed[:TOKENS], to_query[...]).astype(BF16).astype(F32)
    seen = dot(normed, to_context[...]).astype(BF16)
    context[...] = seen[HALF:TOKENS]
    spread_heads(queries[HALF:], spread_query)
    spread_heads(queries[:HALF], spread_here)
    attended[...] = attend(spread_here, seen[:HALF], seen[TOKENS:], True)


def block_kernel(pairs, beyond, folded, query, output, gain, to_context, latent, attended,
                 spread_query, context, mix, second_gain, up, down, out, rows, values, weights, pooled):
    near = lax.axis_index("near")
    band = lax.axis_index("far") * 2 + near
    for step in range(3):
        parts = []
        for level in range(3 * step, min(3 * step + 3, LEVELS)):
            parts += [*single_patches(beyond[level].astype(F32), level), jnp.zeros((PLACES - 3 * PART, 128), F32)]
        parts.append(jnp.zeros((128 - PLACES * (len(parts) // 4), 128), F32))
        rows[step] = jnp.concatenate(parts, axis=0).astype(BF16)
    pool_parts(rows[...].reshape(3 * 128, 128), folded, values, weights, pooled)
    tokens = latent_rows(dot_nt(pick_halo(), pooled[...]), query, output)
    normed = layer_norm(tokens.astype(F32), gain[...]).astype(BF16)
    beside = dot(normed, to_context[...]).astype(BF16)
    there = (band > 0) & (band < 2 * pairs - 1)
    second_half = attend(spread_query, context[...], beside, there)
    both = jnp.concatenate([attended[...], second_half], axis=0)
    mixed = dot(both, mix[...]) + latent[...].astype(F32)
    second = layer_norm(mixed, second_gain[...]).astype(BF16)
    hidden = jax.nn.gelu(dot(second, up[...])).astype(BF16)
    result = mixed + dot(hidden, down[...])
    for half in range(2):
        first_row = (1 - near if half == 0 else near) * 3
        for q in range(LATENT):
            for i in range(3):
                start = half * HALF + (q * 3 + i) * COLS
                out[q, pl.ds(first_row + i, 1)] = result[start : start + COLS].astype(BF16)[None]


def call(kernel, outs, scratch=(), flops=0, moved=0, limit=24, hbm=0, **specs):
    if hbm:
        specs["in_specs"] = [pl.BlockSpec(memory_space=pltpu.HBM)] * hbm
    return pl.pallas_call(
        kernel,
        out_shape=outs,
        scratch_shapes=list(scratch),
        compiler_params=pltpu.CompilerParams(vmem_limit_bytes=limit * 2**20),
        cost_estimate=pl.CostEstimate(flops=flops, bytes_accessed=moved, transcendentals=0),
        **specs,
    )


def shaped(*shape, dtype=BF16):
    return jax.ShapeDtypeStruct(shape, dtype)


def body(
    patches,
    level_bias,
    embed_weight,
    latent_query,
    cross_key,
    cross_value,
    cross_output,
    first_gain,
    window_query,
    window_context,
    window_output,
    second_gain,
    up_weight,
    down_weight,
):
    pairs = lax.axis_size("far")
    blocks = call(
        blocks_kernel,
        shaped(2 * LEVELS, 2 * PART, 256),
        (
            pltpu.VMEM(patches.shape[1:], BF16),
            pltpu.VMEM((ROWS, patches.shape[2] + 128), F32),
            pltpu.VMEM((LEVELS, 2 * PART, 256), F32),
            pltpu.VMEM((LEVELS, 2 * PART, 256), BF16),
            pltpu.SemaphoreType.DMA,
            pltpu.SemaphoreType.DMA((2 * LEVELS,)),
        ),
        flops=10**6,
        moved=10**6,
        hbm=1,
        out_specs=pl.BlockSpec(memory_space=pl.ANY),
    )(pltpu.with_memory_space_constraint(patches, pltpu.HBM))
    x = lax.all_to_all(blocks, ("var", "near"), 0, 0, tiled=True).reshape(LEVELS, 2, 2 * PART, 256)
    folded = call(
        fold_kernel,
        shaped(FOLDED, 128),
        tuple(pltpu.VMEM(a.shape, BF16) for a in (level_bias, embed_weight, latent_query, cross_key, cross_value))
        + (pltpu.SemaphoreType.DMA((5,)),),
        flops=10**9,
        moved=6 * 10**6,
        hbm=5,
    )(
        *(
            pltpu.with_memory_space_constraint(a, pltpu.HBM)
            for a in (level_bias, embed_weight, latent_query, cross_key, cross_value)
        )
    )
    swaps = [(2 * k + 1, 2 * k + 2) for k in range(pairs - 1)]
    swaps += [(b, a) for a, b in swaps]
    near = lax.axis_index("near")
    mine = lax.dynamic_index_in_dim(x, near, 1, keepdims=False)
    mine = jnp.where(near == 1, mine[:, PART:], mine[:, :PART])
    beyond = lax.ppermute(mine, ("far", "near"), swaps)

    def pool_scratch(steps):
        return (
            pltpu.VMEM((steps, 128, 128), BF16),
            pltpu.VMEM((FOLDED, steps * 128), F32),
            pltpu.VMEM((steps, SCORES, 128), F32),
            pltpu.VMEM((D, LATENT * 128), BF16),
        )

    gain = first_gain.reshape(1, D)
    latent, attended, spread_query, context = call(
        own_kernel,
        (shaped(TOKENS, D), shaped(HALF, D), shaped(4, 128, 512), shaped(HALF, 2 * D)),
        (*pool_scratch(LEVELS), pltpu.VMEM((4, 128, 512), BF16)),
        flops=3 * 10**9,
        moved=10**7,
    )(x, folded, latent_query, cross_output, gain, window_query, window_context)
    return call(
        functools.partial(block_kernel, pairs),
        shaped(LATENT, ROWS, COLS, D),
        pool_scratch(3),
        flops=4 * 10**9,
        moved=10**7,
    )(beyond, folded, latent_query, cross_output, gain, window_context, latent, attended, spread_query, context,
      window_output, second_gain.reshape(1, D), up_weight, down_weight)


def solution(mesh):
    finer = Mesh(
        mesh.devices.reshape(mesh.shape["var"], mesh.shape["lat"] // 2, 2, mesh.shape["dp"]),
        ("var", "far", "near", "dp"),
    )
    return jax.shard_map(
        body,
        mesh=finer,
        in_specs=(P(("dp", "var"), ("far", "near"), None),) + (P(),) * 13,
        out_specs=P("dp", ("far", "near"), "var", None),
        check_vma=False,
    )
```

time: 32.2 us -> 30.3 us (0.941)
  Pallas kernels: 13.4 us -> 12.2 us
  waiting for transfers between devices: 4.94 us -> 4.27 us
    pallas_call x1, Pallas kernels: 4.27 us -> 3.11 us  [body(): call(own_kernel, (shaped(TOKENS, D), shaped(HALF, D), shaped(4, 128, 512)...]
    all_to_all x1, waiting for transfers between devices: 4.94 us -> 4.27 us  [body(): lax.all_to_all(blocks, ('var', 'near'), 0, 0, tiled=True)]
    pallas_call x1, Pallas kernels: 5.21 us -> 4.7 us  [body(): call(functools.partial(block_kernel, pairs), shaped(LATENT, ROWS, COLS, D...]
    pallas_call x2, Pallas kernels: 3.95 us -> 4.34 us  [the longest x1 2.38 us: body(): call(fold_kernel, shaped(FOLDED, 128), tuple((pltpu.VMEM(a.shape, BF16) f...]
  transfers between devices with their start and end apart: 2 -> 2, of which waited for: 1 -> 1; matrix products, arithmetic and copies ran while one was open for 0% -> 0% of each run, Pallas kernels for 20% -> 18%
where the time goes in v4:
time: 30.3 us; the launch traced here: 30 us
  starting transfers between devices  13.3 us (44%)
  Pallas kernels  12.2 us (40%)
  waiting for transfers between devices  4.27 us (14%)
    all_to_all x1, starting transfers between devices, body(): lax.all_to_all(blocks, ('var', 'near'), 0, 0, tiled=True)  7.4 us
    ppermute x1, starting transfers between devices, body(): beyond = lax.ppermute(mine, ('far', 'near'), swaps)  5.93 us
    pallas_call x1, Pallas kernels, body(): call(functools.partial(block_kernel, pairs), shaped(LATENT, ROWS, COLS, D...  4.7 us
    all_to_all x1, waiting for transfers between devices, body(): lax.all_to_all(blocks, ('var', 'near'), 0, 0, tiled=True)  4.27 us
    pallas_call x1, Pallas kernels, body(): call(own_kernel, (shaped(TOKENS, D), shaped(HALF, D), shaped(4, 128, 512)...  3.11 us
    pallas_call x1, Pallas kernels, body(): call(fold_kernel, shaped(FOLDED, 128), tuple((pltpu.VMEM(a.shape, BF16) f...  2.38 us
    pallas_call x1, Pallas kernels, body(): call(blocks_kernel, shaped(2 * LEVELS, 2 * PART, 256), (pltpu.VMEM(patche...  1.95 us
  transfers between devices with their start and end apart: 2, of which 1 were waited for; matrix products, arithmetic and copies ran while one was open for 0% of the time, Pallas kernels for 18%

profile of v4, /device:TPU:104, one launch (start us, length us, event | category | flops | bytes accessed | tf_op | source)
XLA Modules:
  0.0 30.0 jit_solution(9589618799217530209)
XLA Ops:
  0.0 2.0 %shard_map.136 = bf16[16,24,256]{2,1,0:T(8,128)(2,1)} custom-call(bf16[1,6,7680]{2,1,0:T(8,128)(2,1)} %pixels.1), custom_call_target="tpu_custom_call" | custom-call | flops 1000000 | bytes 1000000 | tf_op jit(solution)/shard_map/pallas_call | solution.py:328
  2.0 7.4 %all-to-all-start = ((bf16[16,24,256]{2,1,0:T(8,128)(2,1)}), bf16[16,24,256]{2,1,0:T(8,128)(2,1)S(1)}, u32[]{:S(2)}, u32[]{:S(2)}) async-start(bf16[16,24,256]{2,1,0:T(8,128)(2,1)} %shard_map.136), calls=%async_computation | async-start | bytes 393216 | tf_op jit(solution)/shard_map/all_to_all | solution.py:344
  9.4 0.0 copy-start.2
  9.4 0.0 copy-start.3
  9.4 0.0 copy-start.4
  9.4 0.0 copy-start.6
  9.4 0.0 copy-start.7
  9.4 2.4 %shard_map.137.folded = bf16[608,128]{1,0:T(8,128)(2,1)S(1)} custom-call(bf16[8,512]{1,0:T(8,128)(2,1)} %bias_hbm.1, bf16[80,512]{1,0:T(8,128)(2,1)} %embed_hbm.1, bf16[3,512]{1,0:T(4,128)(2,1)} %query.3, bf16[512,512]{1,0:T(8,128)(2,1)} %key_hbm.1, bf16[512,512]{1,0:T(8,128)(2,1)} %value_hbm.1), custom_call_target="tpu_custom_call" | custom-call | flops 1000000000 | bytes 6000000 | tf_op jit(solution)/shard_map/pallas_call | solution.py:345
  11.8 4.3 %all-to-all-done = bf16[16,24,256]{2,1,0:T(8,128)(2,1)S(1)} async-done(((bf16[16,24,256]{2,1,0:T(8,128)(2,1)}), bf16[16,24,256]{2,1,0:T(8,128)(2,1)S(1)}, u32[]{:S(2)}, u32[]{:S(2)}) %all-to-all-start) | async-done | bytes 196640 | tf_op jit(solution)/shard_map/all_to_all | solution.py:344
  16.1 5.9 %collective-permute-start = (bf16[8,12,256]{2,1,0:T(8,128)(2,1)S(1)}, bf16[8,12,256]{2,1,0:T(8,128)(2,1)S(1)}, u32[]{:S(2)}, u32[]{:S(2)}) collective-permute-start(bf16[8,12,256]{2,1,0:T(8,128)(2,1)S(1)} %slice_select_fusion), channel_id=1, source_target_pairs={{2,4},{6,8},{10,12},{14,16},{18,20},{22,24},{26,28},{4,2},{8,6},{1... | collective-permute-start | bytes 147464 | tf_op jit(solution)/shard_map/ppermute | solution.py:364
  22.1 0.0 copy-done.2
  22.1 0.0 copy-done.3
  22.1 0.0 copy-done.4
  22.1 0.0 copy-done.6
  22.1 0.0 copy-done.7
  22.1 0.0 copy-start
  22.1 0.0 copy-start.1
  22.1 0.0 copy-start.5
  22.2 0.0 copy-start.8
  22.2 3.1 %shard_map.138 = (bf16[224,512]{1,0:T(8,128)(2,1)S(1)}, bf16[112,512]{1,0:T(8,128)(2,1)S(1)}, bf16[4,128,512]{2,1,0:T(8,128)(2,1)S(1)}, bf16[112,1024]{1,0:T(8,128)(2,1)S(1)}) custom-call(bf16[8,2,24,256]{3,2,1,0:T(8,128)(2,1)S(1)} %bitcast.6, bf16[608,128]{1,0:T(8,128)(2,1)S(1)} %shard_map.137.folded, bf16[3,512]{1,0:T(4,128)(2,1)S(1)} %copy-done.6, ...), custom_call_target="tpu_custom_call" | custom-call | flops 3000000000 | bytes 10000000 | tf_op jit(solution)/shard_map/pallas_call | solution.py:375
  25.3 0.0 collective-permute-done.beyond
  25.3 0.0 copy-done
  25.3 0.0 copy-done.1
  25.3 0.0 copy-done.5
  25.3 0.0 copy-done.8
  25.3 4.7 %shard_map.139 = bf16[3,6,12,512]{3,2,1,0:T(8,128)(2,1)} custom-call(bf16[8,12,256]{2,1,0:T(8,128)(2,1)S(1)} %collective-permute-done.beyond, bf16[608,128]{1,0:T(8,128)(2,1)S(1)} %shard_map.137.folded, bf16[3,512]{1,0:T(4,128)(2,1)S(1)} %copy-done.6, bf16[512,512]{1,0:T(8,128)(2,1)S(1)} %copy-done.4, f32[1,512]{1,0:T(1,128)S(1)} %bitcast.8, ...), custom_call_target="tpu_custom_call" | custom-call | flops 4000000000 | bytes 10000000 | tf_op jit(solution)/shard_map/pallas_call | solution.py:382
  (2 shorter events, 0.0 us)
Async XLA Ops:
  2.0 14.1 %all-to-all-start = ((bf16[16,24,256]{2,1,0:T(8,128)(2,1)}), bf16[16,24,256]{2,1,0:T(8,128)(2,1)S(1)}, u32[]{:S(2)}, u32[]{:S(2)}) async-start(bf16[16,24,256]{2,1,0:T(8,128)(2,1)} %shard_map.136), calls=%async_computation | async-start | bytes 393216 | tf_op jit(solution)/shard_map/all_to_all | solution.py:344
  9.4 12.7 %copy-start.2 = (bf16[512,1024]{1,0:T(8,128)(2,1)S(1)}, bf16[512,1024]{1,0:T(8,128)(2,1)}, u32[]{:S(2)}) copy-start(bf16[512,1024]{1,0:T(8,128)(2,1)} %to_context.3) | copy-start | bytes 3145732
  9.4 12.7 %copy-start.3 = (bf16[512,512]{1,0:T(8,128)(2,1)S(1)}, bf16[512,512]{1,0:T(8,128)(2,1)}, u32[]{:S(2)}) copy-start(bf16[512,512]{1,0:T(8,128)(2,1)} %to_query.1) | copy-start | bytes 1572868
  9.4 12.7 %copy-start.4 = (bf16[512,512]{1,0:T(8,128)(2,1)S(1)}, bf16[512,512]{1,0:T(8,128)(2,1)}, u32[]{:S(2)}) copy-start(bf16[512,512]{1,0:T(8,128)(2,1)} %output.3) | copy-start | bytes 1572868
  9.4 12.7 %copy-start.6 = (bf16[3,512]{1,0:T(4,128)(2,1)S(1)}, bf16[3,512]{1,0:T(4,128)(2,1)}, u32[]{:S(2)}) copy-start(bf16[3,512]{1,0:T(4,128)(2,1)} %query.3) | copy-start | bytes 9220
  9.4 12.7 %copy-start.7 = (f32[512]{0:T(512)S(1)}, f32[512]{0:T(512)}, u32[]{:S(2)}) copy-start(f32[512]{0:T(512)} %param.21) | copy-start | bytes 6148
  16.1 9.2 %collective-permute-start = (bf16[8,12,256]{2,1,0:T(8,128)(2,1)S(1)}, bf16[8,12,256]{2,1,0:T(8,128)(2,1)S(1)}, u32[]{:S(2)}, u32[]{:S(2)}) collective-permute-start(bf16[8,12,256]{2,1,0:T(8,128)(2,1)S(1)} %slice_select_fusion), channel_id=1, source_target_pairs={{2,4},{6,8},{10,12},{14,16},{18,20},{22,24},{26,28},{4,2},{8,6},{1... | collective-permute-start | bytes 147464 | tf_op jit(solution)/shard_map/ppermute | solution.py:364
  22.1 3.2 %copy-start = (bf16[512,2048]{1,0:T(8,128)(2,1)S(1)}, bf16[512,2048]{1,0:T(8,128)(2,1)}, u32[]{:S(2)}) copy-start(bf16[512,2048]{1,0:T(8,128)(2,1)} %up.1) | copy-start | bytes 6291460
  22.1 3.2 %copy-start.1 = (bf16[2048,512]{1,0:T(8,128)(2,1)S(1)}, bf16[2048,512]{1,0:T(8,128)(2,1)}, u32[]{:S(2)}) copy-start(bf16[2048,512]{1,0:T(8,128)(2,1)} %down.1) | copy-start | bytes 6291460
  22.1 3.2 %copy-start.5 = (bf16[512,512]{1,0:T(8,128)(2,1)S(1)}, bf16[512,512]{1,0:T(8,128)(2,1)}, u32[]{:S(2)}) copy-start(bf16[512,512]{1,0:T(8,128)(2,1)} %mix.1) | copy-start | bytes 1572868
  22.2 3.2 %copy-start.8 = (f32[512]{0:T(512)S(1)}, f32[512]{0:T(512)}, u32[]{:S(2)}) copy-start(f32[512]{0:T(512)} %param.25) | copy-start | bytes 6148

commit v5 on v4

--- a/solution.py
+++ b/solution.py
@@ -55,26 +55,19 @@
     return offset * lax.rsqrt(spread + EPSILON) * scales
 
 
-def blocks_kernel(pixels, out, held, wide, rows, staged, arrived, left):
-    copy = pltpu.make_async_copy(pixels.at[0], held, arrived)
-    copy.start()
-    length = held.shape[1]
+def blocks_kernel(pixels, out, wide, rows):
+    length = pixels.shape[2]
     wide[:, length:] = jnp.zeros((ROWS, 128), F32)
-    copy.wait()
-    wide[:, :length] = held[...].astype(F32)
-    copies = []
+    wide[:, :length] = pixels[0].astype(F32)
     for v in range(LEVELS):
         for group in range(COLS // 3):
             start = (v * COLS + 3 * group) * PIXELS
             patches = wide[:, start : start + 256]
             rows[v, 3 * group : 3 * group + 3] = patches[:3]
             rows[v, PART + 3 * group : PART + 3 * group + 3] = patches[3:]
-        staged[v] = rows[v].astype(BF16)
-        for k in range(2):
-            copies.append(pltpu.make_async_copy(staged.at[v], out.at[2 * v + k], left.at[2 * v + k]))
-            copies[-1].start()
-    for copy in copies:
-        copy.wait()
+        block = rows[v].astype(BF16)
+        out[2 * v] = block
+        out[2 * v + 1] = block
 
 
 def fold_kernel(bias_hbm, embed_hbm, query_hbm, key_hbm, value_hbm, folded, bias, embed, query, key, value, arrived):
@@ -173,7 +166,8 @@
 
 
 def pool_levels(x, folded, values, weights, pooled):
-    values[...] = dot_nt(folded[...], x)
+    for step in range(LEVELS):
+        values[:, step * 128 : (step + 1) * 128] = dot_nt(folded[...], x[step])
     scores = [level_scores(values, step) for step in range(LEVELS)]
     highest = functools.reduce(jnp.maximum, scores)
     shares = [jnp.exp2((score - highest) * RATE) for score in scores]
@@ -249,7 +243,7 @@
         halo = jnp.where(near == 1, other[PART:], other[:PART])
         patches = single_patches(jnp.concatenate([own, halo, jnp.zeros((4, 256), F32)], axis=0), level)
         rows[level] = jnp.concatenate([*patches, jnp.zeros((8, 128), F32)], axis=0).astype(BF16)
-    pool_levels(rows[...].reshape(LEVELS * 128, 128), folded, values, weights, pooled)
+    pool_levels(rows, folded, values, weights, pooled)
     picked = dot_nt(pick_first(near), pooled[...])
     tokens = latent_rows(picked, query, output)
     latent[...] = tokens[:TOKENS]
@@ -263,13 +257,14 @@
 
 
 def block_kernel(pairs, beyond, folded, query, output, gain, to_context, latent, attended,
-                 spread_query, context, mix, second_gain, up, down, out, rows, values, weights, pooled):
+                 spread_query, context, mix, second_gain, up, down, out, rows, values, weights, pooled, staged, left):
     near = lax.axis_index("near")
     band = lax.axis_index("far") * 2 + near
+    wide = beyond[...].astype(F32)
     for step in range(3):
         parts = []
         for level in range(3 * step, min(3 * step + 3, LEVELS)):
-            parts += [*single_patches(beyond[level].astype(F32), level), jnp.zeros((PLACES - 3 * PART, 128), F32)]
+            parts += [*single_patches(wide[level * PART : (level + 1) * PART], level), jnp.zeros((PLACES - 3 * PART, 128), F32)]
         parts.append(jnp.zeros((128 - PLACES * (len(parts) // 4), 128), F32))
         rows[step] = jnp.concatenate(parts, axis=0).astype(BF16)
     pool_parts(rows[...].reshape(3 * 128, 128), folded, values, weights, pooled)
@@ -281,14 +276,20 @@
     both = jnp.concatenate([attended[...], second_half], axis=0)
     mixed = dot(both, mix[...]) + latent[...].astype(F32)
     second = layer_norm(mixed, second_gain[...]).astype(BF16)
-    hidden = jax.nn.gelu(dot(second, up[...])).astype(BF16)
-    result = mixed + dot(hidden, down[...])
+    copies = []
     for half in range(2):
-        first_row = (1 - near if half == 0 else near) * 3
+        own = slice(half * HALF, (half + 1) * HALF)
+        hidden = jax.nn.gelu(dot(second[own], up[...])).astype(BF16)
+        result = mixed[own] + dot(hidden, down[...])
         for q in range(LATENT):
             for i in range(3):
-                start = half * HALF + (q * 3 + i) * COLS
-                out[q, pl.ds(first_row + i, 1)] = result[start : start + COLS].astype(BF16)[None]
+                start = (q * 3 + i) * COLS
+                staged[half, q, i] = result[start : start + COLS].astype(BF16)
+        first_row = 3 - 3 * near if half == 0 else 3 * near
+        copies.append(pltpu.make_async_copy(staged.at[half], out.at[:, pl.ds(first_row, 3)], left.at[half]))
+        copies[-1].start()
+    for copy in copies:
+        copy.wait()
 
 
 def call(kernel, outs, scratch=(), flops=0, moved=0, limit=24, hbm=0, **specs):
@@ -328,19 +329,10 @@
     blocks = call(
         blocks_kernel,
         shaped(2 * LEVELS, 2 * PART, 256),
-        (
-            pltpu.VMEM(patches.shape[1:], BF16),
-            pltpu.VMEM((ROWS, patches.shape[2] + 128), F32),
-            pltpu.VMEM((LEVELS, 2 * PART, 256), F32),
-            pltpu.VMEM((LEVELS, 2 * PART, 256), BF16),
-            pltpu.SemaphoreType.DMA,
-            pltpu.SemaphoreType.DMA((2 * LEVELS,)),
-        ),
+        (pltpu.VMEM((ROWS, patches.shape[2] + 128), F32), pltpu.VMEM((LEVELS, 2 * PART, 256), F32)),
         flops=10**6,
         moved=10**6,
-        hbm=1,
-        out_specs=pl.BlockSpec(memory_space=pl.ANY),
-    )(pltpu.with_memory_space_constraint(patches, pltpu.HBM))
+    )(patches)
     x = lax.all_to_all(blocks, ("var", "near"), 0, 0, tiled=True).reshape(LEVELS, 2, 2 * PART, 256)
     folded = call(
         fold_kernel,
@@ -360,7 +352,7 @@
     swaps += [(b, a) for a, b in swaps]
     near = lax.axis_index("near")
     mine = lax.dynamic_index_in_dim(x, near, 1, keepdims=False)
-    mine = jnp.where(near == 1, mine[:, PART:], mine[:, :PART])
+    mine = jnp.where(near == 1, mine[:, PART:], mine[:, :PART]).reshape(LEVELS * PART, 256)
     beyond = lax.ppermute(mine, ("far", "near"), swaps)
 
     def pool_scratch(steps):
@@ -382,9 +374,10 @@
     return call(
         functools.partial(block_kernel, pairs),
         shaped(LATENT, ROWS, COLS, D),
-        pool_scratch(3),
+        (*pool_scratch(3), pltpu.VMEM((2, LATENT, 3, COLS, D), BF16), pltpu.SemaphoreType.DMA((2,))),
         flops=4 * 10**9,
         moved=10**7,
+        out_specs=pl.BlockSpec(memory_space=pl.ANY),
     )(beyond, folded, latent_query, cross_output, gain, window_context, latent, attended, spread_query, context,
       window_output, second_gain.reshape(1, D), up_weight, down_weight)
 

time: 30.3 us -> 30.1 us (level)
  Pallas kernels: 12.2 us -> 11.1 us
  local copies, waits for them, and re-layouts: 0.06 us -> 0.98 us
    pallas_call x1, Pallas kernels: 1.95 us -> 0.88 us  [body(): call(blocks_kernel, shaped(2 * LEVELS, 2 * PART, 256), (pltpu.VMEM((ROWS,...]
    unnamed x18 -> x20, local copies, waits for them, and re-layouts: 0.05 us -> 0.96 us
where the time goes in v5:
time: 30.1 us; the launch traced here: 29.9 us
  starting transfers between devices  13.3 us (44%)
  Pallas kernels  11.1 us (37%)
  waiting for transfers between devices  4.27 us (14%)
  local copies, waits for them, and re-layouts  0.98 us (3%)
    all_to_all x1, starting transfers between devices, body(): lax.all_to_all(blocks, ('var', 'near'), 0, 0, tiled=True)  7.39 us
    ppermute x1, starting transfers between devices, body(): beyond = lax.ppermute(mine, ('far', 'near'), swaps)  5.93 us
    pallas_call x1, Pallas kernels, body(): call(functools.partial(block_kernel, pairs), shaped(LATENT, ROWS, COLS, D...  4.7 us
    all_to_all x1, waiting for transfers between devices, body(): lax.all_to_all(blocks, ('var', 'near'), 0, 0, tiled=True)  4.27 us
    pallas_call x1, Pallas kernels, body(): call(own_kernel, (shaped(TOKENS, D), shaped(HALF, D), shaped(4, 128, 512)...  3.1 us
    pallas_call x1, Pallas kernels, body(): call(fold_kernel, shaped(FOLDED, 128), tuple((pltpu.VMEM(a.shape, BF16) f...  2.38 us
    unnamed x20, local copies, waits for them, and re-layouts  0.96 us
    pallas_call x1, Pallas kernels, body(): call(blocks_kernel, shaped(2 * LEVELS, 2 * PART, 256), (pltpu.VMEM((ROWS,...  0.88 us
  transfers between devices with their start and end apart: 2, of which 1 were waited for; matrix products, arithmetic and copies ran while one was open for 0% of the time, Pallas kernels for 18%

profile of v5, /device:TPU:104, one launch (start us, length us, event | category | flops | bytes accessed | tf_op | source)
XLA Modules:
  0.0 29.9 jit_solution(9371588576390147018)
XLA Ops:
  0.0 0.0 copy-start
  0.0 0.9 %copy-done = bf16[1,6,7680]{2,1,0:T(8,128)(2,1)S(1)} copy-done((bf16[1,6,7680]{2,1,0:T(8,128)(2,1)S(1)}, bf16[1,6,7680]{2,1,0:T(8,128)(2,1)}, u32[]{:S(2)}) %copy-start) | copy-done | bytes 92184
  0.9 0.9 %shard_map.136 = bf16[16,24,256]{2,1,0:T(8,128)(2,1)} custom-call(bf16[1,6,7680]{2,1,0:T(8,128)(2,1)S(1)} %copy-done), custom_call_target="tpu_custom_call" | custom-call | flops 1000000 | bytes 1000000 | tf_op jit(solution)/shard_map/pallas_call | solution.py:329
  1.8 7.4 %all-to-all-start = ((bf16[16,24,256]{2,1,0:T(8,128)(2,1)}), bf16[16,24,256]{2,1,0:T(8,128)(2,1)S(1)}, u32[]{:S(2)}, u32[]{:S(2)}) async-start(bf16[16,24,256]{2,1,0:T(8,128)(2,1)} %shard_map.136), calls=%async_computation | async-start | bytes 393216 | tf_op jit(solution)/shard_map/all_to_all | solution.py:336
  9.2 0.0 copy-start.3
  9.2 0.0 copy-start.4
  9.2 0.0 copy-start.5
  9.2 0.0 copy-start.7
  9.2 0.0 copy-start.8
  9.2 2.4 %shard_map.137.folded = bf16[608,128]{1,0:T(8,128)(2,1)S(1)} custom-call(bf16[8,512]{1,0:T(8,128)(2,1)} %bias_hbm.1, bf16[80,512]{1,0:T(8,128)(2,1)} %embed_hbm.1, bf16[3,512]{1,0:T(4,128)(2,1)} %query.3, bf16[512,512]{1,0:T(8,128)(2,1)} %key_hbm.1, bf16[512,512]{1,0:T(8,128)(2,1)} %value_hbm.1), custom_call_target="tpu_custom_call" | custom-call | flops 1000000000 | bytes 6000000 | tf_op jit(solution)/shard_map/pallas_call | solution.py:337
  11.6 4.3 %all-to-all-done = bf16[16,24,256]{2,1,0:T(8,128)(2,1)S(1)} async-done(((bf16[16,24,256]{2,1,0:T(8,128)(2,1)}), bf16[16,24,256]{2,1,0:T(8,128)(2,1)S(1)}, u32[]{:S(2)}, u32[]{:S(2)}) %all-to-all-start) | async-done | bytes 196640 | tf_op jit(solution)/shard_map/all_to_all | solution.py:336
  16.0 5.9 %collective-permute-start = (bf16[96,256]{1,0:T(8,128)(2,1)S(1)}, bf16[96,256]{1,0:T(8,128)(2,1)S(1)}, u32[]{:S(2)}, u32[]{:S(2)}) collective-permute-start(bf16[96,256]{1,0:T(8,128)(2,1)S(1)} %reshape.13), channel_id=1, source_target_pairs={{2,4},{6,8},{10,12},{14,16},{18,20},{22,24},{26,28},{4,2},{8,6},{1... | collective-permute-start | bytes 147464 | tf_op jit(solution)/shard_map/ppermute | solution.py:356
  21.9 0.0 copy-done.3
  21.9 0.0 copy-done.4
  21.9 0.0 copy-done.5
  21.9 0.0 copy-done.7
  21.9 0.0 copy-done.8
  21.9 0.0 copy-start.1
  22.0 0.0 copy-start.2
  22.0 0.0 copy-start.6
  22.0 0.0 copy-start.9
  22.0 3.1 %shard_map.138 = (bf16[224,512]{1,0:T(8,128)(2,1)S(1)}, bf16[112,512]{1,0:T(8,128)(2,1)S(1)}, bf16[4,128,512]{2,1,0:T(8,128)(2,1)S(1)}, bf16[112,1024]{1,0:T(8,128)(2,1)S(1)}) custom-call(bf16[8,2,24,256]{3,2,1,0:T(8,128)(2,1)S(1)} %bitcast.6, bf16[608,128]{1,0:T(8,128)(2,1)S(1)} %shard_map.137.folded, bf16[3,512]{1,0:T(4,128)(2,1)S(1)} %copy-done.7, ...), custom_call_target="tpu_custom_call" | custom-call | flops 3000000000 | bytes 10000000 | tf_op jit(solution)/shard_map/pallas_call | solution.py:367
  25.1 0.0 collective-permute-done.beyond
  25.1 0.0 copy-done.1
  25.1 0.0 copy-done.2
  25.1 0.0 copy-done.6
  25.1 0.0 copy-done.9
  25.2 4.7 %shard_map.139 = bf16[3,6,12,512]{3,2,1,0:T(8,128)(2,1)} custom-call(bf16[96,256]{1,0:T(8,128)(2,1)S(1)} %collective-permute-done.beyond, bf16[608,128]{1,0:T(8,128)(2,1)S(1)} %shard_map.137.folded, bf16[3,512]{1,0:T(4,128)(2,1)S(1)} %copy-done.7, bf16[512,512]{1,0:T(8,128)(2,1)S(1)} %copy-done.5, f32[1,512]{1,0:T(1,128)S(1)} %bitcast.8, ...), custom_call_target="tpu_custom_call" | custom-call | flops 4000000000 | bytes 10000000 | tf_op jit(solution)/shard_map/pallas_call | solution.py:374
  (3 shorter events, 0.0 us)
Async XLA Ops:
  0.0 0.9 %copy-start = (bf16[1,6,7680]{2,1,0:T(8,128)(2,1)S(1)}, bf16[1,6,7680]{2,1,0:T(8,128)(2,1)}, u32[]{:S(2)}) copy-start(bf16[1,6,7680]{2,1,0:T(8,128)(2,1)} %pixels.1) | copy-start | bytes 276484
  1.8 14.1 %all-to-all-start = ((bf16[16,24,256]{2,1,0:T(8,128)(2,1)}), bf16[16,24,256]{2,1,0:T(8,128)(2,1)S(1)}, u32[]{:S(2)}, u32[]{:S(2)}) async-start(bf16[16,24,256]{2,1,0:T(8,128)(2,1)} %shard_map.136), calls=%async_computation | async-start | bytes 393216 | tf_op jit(solution)/shard_map/all_to_all | solution.py:336
  9.2 12.7 %copy-start.3 = (bf16[512,1024]{1,0:T(8,128)(2,1)S(1)}, bf16[512,1024]{1,0:T(8,128)(2,1)}, u32[]{:S(2)}) copy-start(bf16[512,1024]{1,0:T(8,128)(2,1)} %to_context.3) | copy-start | bytes 3145732
  9.2 12.7 %copy-start.4 = (bf16[512,512]{1,0:T(8,128)(2,1)S(1)}, bf16[512,512]{1,0:T(8,128)(2,1)}, u32[]{:S(2)}) copy-start(bf16[512,512]{1,0:T(8,128)(2,1)} %to_query.1) | copy-start | bytes 1572868
  9.2 12.7 %copy-start.5 = (bf16[512,512]{1,0:T(8,128)(2,1)S(1)}, bf16[512,512]{1,0:T(8,128)(2,1)}, u32[]{:S(2)}) copy-start(bf16[512,512]{1,0:T(8,128)(2,1)} %output.3) | copy-start | bytes 1572868
  9.2 12.7 %copy-start.7 = (bf16[3,512]{1,0:T(4,128)(2,1)S(1)}, bf16[3,512]{1,0:T(4,128)(2,1)}, u32[]{:S(2)}) copy-start(bf16[3,512]{1,0:T(4,128)(2,1)} %query.3) | copy-start | bytes 9220
  9.2 12.7 %copy-start.8 = (f32[512]{0:T(512)S(1)}, f32[512]{0:T(512)}, u32[]{:S(2)}) copy-start(f32[512]{0:T(512)} %param.21) | copy-start | bytes 6148
  16.0 9.1 %collective-permute-start = (bf16[96,256]{1,0:T(8,128)(2,1)S(1)}, bf16[96,256]{1,0:T(8,128)(2,1)S(1)}, u32[]{:S(2)}, u32[]{:S(2)}) collective-permute-start(bf16[96,256]{1,0:T(8,128)(2,1)S(1)} %reshape.13), channel_id=1, source_target_pairs={{2,4},{6,8},{10,12},{14,16},{18,20},{22,24},{26,28},{4,2},{8,6},{1... | collective-permute-start | bytes 147464 | tf_op jit(solution)/shard_map/ppermute | solution.py:356
  21.9 3.2 %copy-start.1 = (bf16[512,2048]{1,0:T(8,128)(2,1)S(1)}, bf16[512,2048]{1,0:T(8,128)(2,1)}, u32[]{:S(2)}) copy-start(bf16[512,2048]{1,0:T(8,128)(2,1)} %up.1) | copy-start | bytes 6291460
  22.0 3.2 %copy-start.2 = (bf16[2048,512]{1,0:T(8,128)(2,1)S(1)}, bf16[2048,512]{1,0:T(8,128)(2,1)}, u32[]{:S(2)}) copy-start(bf16[2048,512]{1,0:T(8,128)(2,1)} %down.1) | copy-start | bytes 6291460
  22.0 3.2 %copy-start.6 = (bf16[512,512]{1,0:T(8,128)(2,1)S(1)}, bf16[512,512]{1,0:T(8,128)(2,1)}, u32[]{:S(2)}) copy-start(bf16[512,512]{1,0:T(8,128)(2,1)} %mix.1) | copy-start | bytes 1572868
  22.0 3.2 %copy-start.9 = (f32[512]{0:T(512)S(1)}, f32[512]{0:T(512)}, u32[]{:S(2)}) copy-start(f32[512]{0:T(512)} %param.25) | copy-start | bytes 6148
